TPU v7x, 256 devices: a whole 4x4x8 slice. The times are simulated.
256 devices in a mesh: wide: 32 (over y, x, core), narrow: 8 (over z).
Axes of the slice: x: 4, y: 4, z: 8, core: 2. Of those that a mesh axis runs over, the one named last changes fastest.
Arguments:
- points: float32 [262144, 128], P(('wide', 'narrow'))
- start_basis: float32 [32, 786432], P(None, ('wide', 'narrow')), may hold values from -6 to 6
Outputs:
- embedding: float32 [32, 262144], P(None, ('wide', 'narrow'))
All inputs are finite; a program needn't handle non-finite values.
Results may differ from a plain program's by a relative error of at most 0.0003.
Values sent between devices are 32-bit elements; how exact they have to be, the bound alone decides.
A program may use at most 256 MiB of HBM per device.

v0:
```python
import jax
import jax.numpy as jnp
from jax import lax
from jax.sharding import PartitionSpec as P

ITERS = 4
NS_STEPS = 16


HIGHEST_PRECISION = lax.Precision.HIGHEST


def shifted(value, axis, by):
    devices = lax.axis_size(axis)
    pairs = [(i, i + by) for i in range(devices) if 0 <= i + by < devices]
    return lax.ppermute(value, axis, pairs)


def extended(cells, sides, width, closed):
    for axis, dim in sides:
        count = lax.axis_size(axis)
        ends = count if closed else count - 1
        head = lax.slice_in_dim(cells, 0, width, axis=dim)
        tail = lax.slice_in_dim(cells, cells.shape[dim] - width, cells.shape[dim], axis=dim)
        cells = jnp.concatenate(
            [
                lax.ppermute(tail, axis, [(i, (i + 1) % count) for i in range(ends)]),
                cells,
                lax.ppermute(head, axis, [((i + 1) % count, i) for i in range(ends)]),
            ],
            axis=dim,
        )
    return cells


def from_behind(value, axis, by):
    devices = lax.axis_size(axis)
    return lax.ppermute(value, axis, [(i, (i + by) % devices) for i in range(devices)])


def orthonormal(basis_in):
    covariance = jnp.dot(basis_in, basis_in.T, precision=HIGHEST_PRECISION)
    cholesky_factor = jnp.linalg.cholesky(covariance)
    return jax.scipy.linalg.solve_triangular(cholesky_factor, basis_in, lower=True)


def build_operator(patch_rows):
    total_rows = patch_rows.shape[0]
    step_rows = 192
    kernel_width = 0.5 * patch_rows.shape[1]
    norms = jnp.sum(patch_rows * patch_rows, axis=1)

    def kernel_block(row_start):
        rows_part = lax.dynamic_slice_in_dim(patch_rows, row_start, step_rows, 0)
        norms_part = lax.dynamic_slice_in_dim(norms, row_start, step_rows, 0)
        products = jnp.einsum("bd,pd->bp", rows_part, patch_rows, precision=HIGHEST_PRECISION)
        return jnp.exp(-(norms_part[:, None] + norms[None, :] - 2.0 * products) / kernel_width)

    starts = jnp.arange(total_rows // step_rows, dtype=jnp.int32) * step_rows
    kernel = lax.map(kernel_block, starts).reshape(total_rows, total_rows)
    kernel = kernel - jnp.mean(kernel, axis=0, keepdims=True)
    kernel = kernel - jnp.mean(kernel, axis=1, keepdims=True)
    return 0.5 * kernel


def procrustes(target, source):
    target_mean = jnp.mean(target, axis=1, keepdims=True)
    source_mean = jnp.mean(source, axis=1, keepdims=True)
    covariance = jnp.dot(
        source - source_mean, (target - target_mean).T, precision=HIGHEST_PRECISION
    )
    orthogonal = covariance / jnp.sqrt(jnp.sum(covariance * covariance) + 1e-06)
    for iteration in range(NS_STEPS):
        square = jnp.dot(orthogonal, orthogonal.T, precision=HIGHEST_PRECISION)
        orthogonal = 1.5 * orthogonal - 0.5 * jnp.dot(
            square, orthogonal, precision=HIGHEST_PRECISION
        )
    translation = target_mean[:, 0] - jnp.dot(
        orthogonal.T, source_mean[:, 0], precision=HIGHEST_PRECISION
    )
    return (orthogonal, translation)


def compose(earlier, later_map):
    rot_early, off_early = earlier
    rot_late, off_late = later_map
    rotation = jnp.einsum("...ij,...jk->...ik", rot_late, rot_early, precision=HIGHEST_PRECISION)
    offset = (
        jnp.einsum("...ji,...j->...i", rot_early, off_late, precision=HIGHEST_PRECISION) + off_early
    )
    return (rotation, offset)


def apply_map(mapping, columns):
    rotation, offset = mapping
    return jnp.dot(rotation.T, columns, precision=HIGHEST_PRECISION) + offset[:, None]


def doubling_step(running, distance, position):
    incoming = shifted((running[0], running[1]), ("wide", "narrow"), distance)
    joined = compose(incoming, running)
    valid = position >= distance
    return (jnp.where(valid, joined[0], running[0]), jnp.where(valid, joined[1], running[1]))


def shards(points, start_basis):
    devices = lax.axis_size(("wide", "narrow"))
    position = lax.axis_index(("wide", "narrow"))
    block_rows = points.shape[0]
    emb_dims = start_basis.shape[0]
    at_start = position == 0
    at_end = position == devices - 1
    identity_rot = jnp.eye(emb_dims, dtype=jnp.float32)
    no_shift = jnp.zeros((emb_dims,), jnp.float32)
    patch_rows = extended(points, ((("wide", "narrow"), 0),), block_rows, True)
    operator = build_operator(patch_rows)
    basis_rows = orthonormal(start_basis)
    for iteration in range(ITERS):
        projected = jnp.dot(basis_rows, operator, precision=HIGHEST_PRECISION)
        if iteration + 1 < ITERS:
            basis_rows = orthonormal(projected)
    embedded = projected / (jnp.sum(projected * projected, axis=1, keepdims=True) + 1e-06) ** 0.25
    prior = from_behind(embedded[:, block_rows:], ("wide", "narrow"), 1)
    rotation, offset = procrustes(prior, embedded[:, : 2 * block_rows])
    earlier = shifted((rotation, offset), ("wide", "narrow"), 1)
    running = (
        jnp.where(at_start, identity_rot, earlier[0]),
        jnp.where(at_start, no_shift, earlier[1]),
    )
    for level in range((devices - 1).bit_length()):
        running = doubling_step(running, 1 << level, position)
    composite = compose(running, (rotation, offset))
    aligned = apply_map(composite, embedded)
    aligned_cols = extended(aligned, ((("wide", "narrow"), 1),), block_rows, False)
    from_prev = aligned_cols[:, :block_rows]
    from_next = aligned_cols[:, -block_rows:]
    has_prev = jnp.where(at_start, 0.0, 1.0).astype(jnp.float32)
    has_next = jnp.where(at_end, 0.0, 1.0).astype(jnp.float32)
    summed = aligned[:, block_rows : 2 * block_rows] + has_prev * from_prev + has_next * from_next
    return summed / (1.0 + has_prev + has_next)


def solution(mesh):
    placed = (P(("wide", "narrow"), None), P(None, ("wide", "narrow")))
    return jax.shard_map(
        shards, mesh=mesh, in_specs=placed, out_specs=P(None, ("wide", "narrow")), check_vma=False
    )
```

profile of v0, /device:TPU:16, one launch (start us, length us, event | category | flops | bytes accessed | tf_op | source)
XLA Modules:
  0.0 416.5 jit_solution(12436227625145858556)
XLA Ops:
  0.0 1.9 collective-permute-start
  1.9 5.6 %collective-permute-start.1 = (f32[1024,128]{1,0:T(8,128)}, f32[1024,128]{1,0:T(8,128)S(1)}, u32[]{:S(2)}, u32[]{:S(2)}) collective-permute-start(f32[1024,128]{1,0:T(8,128)} %param.7), channel_id=1, source_target_pairs={{1,0},{2,1},{3,2},{4,3},{5,4},{6,5},{7,6},{8,7},{9,8},{10,9},{11,1... | collective-permute-start | bytes 1572872 | tf_op jit(solution)/shard_map/ppermute | solution.py:29
  8.0 2.9 cholesky.74
  12.3 2.4 custom-call.8
  15.3 4.0 collective-permute-done
  20.9 102.4 %while.10 = (s32[]{:T(128)}, f32[16,192,3072]{2,1,0:T(8,128)}, s32[16]{0:T(128)S(1)}, f32[3072]{0:T(1024)S(1)}, f32[3072,128]{1,0:T(8,128)S(1)}, /*index=5*/s32[]{:T(128)}, s32[]{:T(128)}, s32[]{:T(128)}) while((s32[]{:T(128)}, f32[16,192,3072]{2,1,0:T(8,128)}, s32[16]{0:T(128)S(1)}, f32[3072]{0:T(1024)S(1)}, f32[3072,128]{1,0:T(8,128)S(1)}, ...), condition=%wide.region_4.0_spmd, body=%wide.region_3.0_spmd.sunk | while | flops 908918784 | bytes 4045963 | solution.py:60
  23.5 3.8 fusion.226
  29.8 3.8 fusion.226
  36.2 3.9 fusion.226
  42.6 3.9 fusion.226
  49.0 3.8 fusion.226
  55.4 3.9 fusion.226
  61.9 3.8 fusion.226
  68.2 3.8 fusion.226
  74.6 3.8 fusion.226
  81.0 3.9 fusion.226
  87.4 3.9 fusion.226
  93.9 3.8 fusion.226
  100.2 3.9 fusion.226
  106.7 3.8 fusion.226
  113.1 3.8 fusion.226
  119.5 3.9 fusion.226
  123.3 13.4 %reduce_sum.64 = f32[3072]{0:T(1024)S(1)} reduce(f32[16,192,3072]{2,1,0:T(8,128)} %get-tuple-element.34, f32[]{:T(128)} %constant.81.clone.1), dimensions={0,1}, to_apply=%region_5.8 | reduce | flops 9434112 | bytes 37761028 | tf_op jit(solution)/shard_map/reduce_sum | solution.py:61
  136.8 14.5 %subtract_reduce_fusion = f32[16,192]{1,0:T(8,128)S(1)} fusion(f32[16,192,3072]{2,1,0:T(8,128)} %get-tuple-element.34, f32[3072]{0:T(1024)S(1)} %broadcast_multiply_fusion.1), kind=kLoop, calls=%fused_computation.12 | loop fusion | flops 18871296 | bytes 37773312 | tf_op jit(solution)/shard_map/reduce_sum | solution.py:62
  151.3 27.7 %fusion.9 = f32[3072,3072]{1,0:T(8,128)} fusion(f32[16,192,3072]{2,1,0:T(8,128)} %get-tuple-element.34, f32[3072]{0:T(1024)S(1)} %div.55, f32[3072]{0:T(1024)S(1)} %broadcast_multiply_fusion.1), kind=kLoop, calls=%fused_computation.11 | loop fusion | flops 28311552 | bytes 75522048 | tf_op jit(solution)/shard_map/mul | solution.py:63
  179.0 25.2 %fusion.104 = f32[32,3072]{1,0:T(8,128)S(1)} fusion(f32[32,3072]{1,0:T(8,128)S(1)} %fusion.72, f32[3072,3072]{1,0:T(8,128)} %fusion.9), kind=kOutput, calls=%fused_computation.185 | convolution fusion | flops 3623878656 | bytes 38535168 | tf_op jit(solution)/shard_map/dot_general | solution.py:119
  204.8 2.9 cholesky.85
  209.0 2.4 custom-call.9
  212.0 25.4 %fusion.106 = f32[32,3072]{1,0:T(8,128)S(1)} fusion(f32[32,3072]{1,0:T(8,128)S(1)} %fusion.69, f32[3072,3072]{1,0:T(8,128)} %fusion.9), kind=kOutput, calls=%fused_computation.187 | convolution fusion | flops 3623878656 | bytes 38535168 | tf_op jit(solution)/shard_map/dot_general | solution.py:119
  238.0 2.9 cholesky.96
  242.2 2.4 custom-call.10
  245.2 25.5 %fusion.108 = f32[32,3072]{1,0:T(8,128)S(1)} fusion(f32[32,3072]{1,0:T(8,128)S(1)} %fusion.66, f32[3072,3072]{1,0:T(8,128)} %fusion.9), kind=kOutput, calls=%fused_computation.189 | convolution fusion | flops 3623878656 | bytes 38535168 | tf_op jit(solution)/shard_map/dot_general | solution.py:119
  271.2 2.9 cholesky.107
  275.5 2.4 custom-call.11
  278.5 25.4 %multiply_reduce_fusion.1 = (f32[32]{0:T(128)S(1)}, f32[32,3072]{1,0:T(8,128)S(1)}) fusion(f32[32,3072]{1,0:T(8,128)S(1)} %fusion.63, f32[3072,3072]{1,0:T(8,128)} %fusion.9), kind=kOutput, calls=%fused_computation.72 | convolution fusion | flops 3624075264 | bytes 38535296 | tf_op jit(solution)/shard_map/dot_general | solution.py:119
  304.3 10.6 %collective-permute-done.2 = f32[32,2048]{1,0:T(8,128)S(1)} collective-permute-done((f32[32,2048]{1,0:T(8,128)S(1)}, f32[32,2048]{1,0:T(8,128)S(1)}, u32[]{:S(2)}, u32[]{:S(2)}) %collective-permute-start.2) | collective-permute-done | bytes 262176 | tf_op jit(solution)/shard_map/ppermute | solution.py:38
  321.7 1.9 collective-permute-start.3
  323.8 1.9 collective-permute-start.12
  325.7 5.3 %collective-permute-done.3 = f32[32,32]{1,0:T(8,128)S(1)} collective-permute-done((f32[32,32]{1,0:T(8,128)S(1)}, f32[32,32]{1,0:T(8,128)S(1)}, u32[]{:S(2)}, u32[]{:S(2)}) %collective-permute-start.3) | collective-permute-done | bytes 4128 | tf_op jit(solution)/shard_map/ppermute | solution.py:16
  331.0 1.9 collective-permute-start.4
  332.9 1.9 collective-permute-start.13
  334.9 5.4 %collective-permute-done.4 = f32[32,32]{1,0:T(8,128)S(1)} collective-permute-done((f32[32,32]{1,0:T(8,128)S(1)}, f32[32,32]{1,0:T(8,128)S(1)}, u32[]{:S(2)}, u32[]{:S(2)}) %collective-permute-start.4) | collective-permute-done | bytes 4128 | tf_op jit(solution)/shard_map/ppermute | solution.py:16
  340.4 1.9 collective-permute-start.5
  342.5 1.9 collective-permute-start.14
  344.4 6.2 %collective-permute-done.5 = f32[32,32]{1,0:T(8,128)S(1)} collective-permute-done((f32[32,32]{1,0:T(8,128)S(1)}, f32[32,32]{1,0:T(8,128)S(1)}, u32[]{:S(2)}, u32[]{:S(2)}) %collective-permute-start.5) | collective-permute-done | bytes 4128 | tf_op jit(solution)/shard_map/ppermute | solution.py:16
  350.7 1.9 collective-permute-start.6
  352.8 1.9 collective-permute-start.15
  354.7 8.0 %collective-permute-done.6 = f32[32,32]{1,0:T(8,128)S(1)} collective-permute-done((f32[32,32]{1,0:T(8,128)S(1)}, f32[32,32]{1,0:T(8,128)S(1)}, u32[]{:S(2)}, u32[]{:S(2)}) %collective-permute-start.6) | collective-permute-done | bytes 4128 | tf_op jit(solution)/shard_map/ppermute | solution.py:16
  362.9 1.9 collective-permute-start.7
  364.9 1.9 collective-permute-start.16
  366.9 3.2 collective-permute-done.7
  370.2 1.9 collective-permute-start.8
  372.2 1.9 collective-permute-start.17
  374.2 3.7 collective-permute-done.8
  378.0 4.0 collective-permute-start.9
  382.2 4.5 %collective-permute-start.18 = (f32[32]{0:T(128)S(1)}, f32[32]{0:T(128)S(1)}, u32[]{:S(2)}, u32[]{:S(2)}) collective-permute-start(f32[32]{0:T(128)S(1)} %fusion.30), channel_id=1, source_target_pairs={{0,32},{1,33},{2,34},{3,35},{4,36},{5,37},{6,38},{7,39},{8,40},{9,... | collective-permute-start | bytes 392 | tf_op jit(solution)/shard_map/ppermute | solution.py:16
  386.8 3.0 collective-permute-start.10
  390.2 1.9 collective-permute-start.19
  393.9 1.7 collective-permute-done.19
  397.0 2.7 collective-permute-done.11
  400.0 2.6 collective-permute-done.20
  403.5 1.9 collective-permute-start.21
  405.4 7.9 %collective-permute-start.22 = (f32[32,1024]{1,0:T(8,128)S(1)}, f32[32,1024]{1,0:T(8,128)S(1)}, u32[]{:S(2)}, u32[]{:S(2)}) collective-permute-start(f32[32,1024]{1,0:T(8,128)S(1)} %get-tuple-element.46), channel_id=1, source_target_pairs={{1,0},{2,1},{3,2},{4,3},{5,4},{6,5},{7,6},{8,7},{9,8},{10,9},{11,1... | collective-permute-start | bytes 393224 | tf_op jit(solution)/shard_map/ppermute | solution.py:29
  414.0 1.8 collective-permute-done.22
  (150 shorter events, 36.1 us)
Async XLA Ops:
  0.0 7.5 %copy-start = (f32[32,3072]{1,0:T(8,128)S(1)}, f32[32,3072]{1,0:T(8,128)}, u32[]{:S(2)}) copy-start(f32[32,3072]{1,0:T(8,128)} %param.8) | copy-start | bytes 1179652
  0.0 19.2 %collective-permute-start = (f32[1024,128]{1,0:T(8,128)}, f32[1024,128]{1,0:T(8,128)S(1)}, u32[]{:S(2)}, u32[]{:S(2)}) collective-permute-start(f32[1024,128]{1,0:T(8,128)} %param.7), channel_id=1, source_target_pairs={{0,1},{1,2},{2,3},{3,4},{4,5},{5,6},{6,7},{7,8},{8,9},{9,10},{10,1... | collective-permute-start | bytes 1572872 | tf_op jit(solution)/shard_map/ppermute | solution.py:27
  1.9 18.4 %collective-permute-start.1 = (f32[1024,128]{1,0:T(8,128)}, f32[1024,128]{1,0:T(8,128)S(1)}, u32[]{:S(2)}, u32[]{:S(2)}) collective-permute-start(f32[1024,128]{1,0:T(8,128)} %param.7), channel_id=1, source_target_pairs={{1,0},{2,1},{3,2},{4,3},{5,4},{6,5},{7,6},{8,7},{9,8},{10,9},{11,1... | collective-permute-start | bytes 1572872 | tf_op jit(solution)/shard_map/ppermute | solution.py:29
  244.7 171.8 %copy-start.1 = (f32[32,3072]{1,0:T(8,128)S(1)}, f32[32,3072]{1,0:T(8,128)}, u32[]{:S(2)}) copy-start(f32[32,3072]{1,0:T(8,128)} %param.8) | copy-start | bytes 1179652
  304.1 10.7 %collective-permute-start.2 = (f32[32,2048]{1,0:T(8,128)S(1)}, f32[32,2048]{1,0:T(8,128)S(1)}, u32[]{:S(2)}, u32[]{:S(2)}) collective-permute-start(f32[32,2048]{1,0:T(8,128)S(1)} %get-tuple-element.48), channel_id=1, source_target_pairs={{0,1},{1,2},{2,3},{3,4},{4,5},{5,6},{6,7},{7,8},{8,9},{9,10},{10,1... | collective-permute-start | bytes 786440 | tf_op jit(solution)/shard_map/ppermute | solution.py:38
  321.7 9.3 %collective-permute-start.3 = (f32[32,32]{1,0:T(8,128)S(1)}, f32[32,32]{1,0:T(8,128)S(1)}, u32[]{:S(2)}, u32[]{:S(2)}) collective-permute-start(f32[32,32]{1,0:T(8,128)S(1)} %get-tuple-element.61), channel_id=1, source_target_pairs={{0,1},{1,2},{2,3},{3,4},{4,5},{5,6},{6,7},{7,8},{8,9},{9,10},{10,1... | collective-permute-start | bytes 12296 | tf_op jit(solution)/shard_map/ppermute | solution.py:16
  323.8 9.1 %collective-permute-start.12 = (f32[32]{0:T(128)S(1)}, f32[32]{0:T(128)S(1)}, u32[]{:S(2)}, u32[]{:S(2)}) collective-permute-start(f32[32]{0:T(128)S(1)} %fusion.25), channel_id=1, source_target_pairs={{0,1},{1,2},{2,3},{3,4},{4,5},{5,6},{6,7},{7,8},{8,9},{9,10},{10,1... | collective-permute-start | bytes 392 | tf_op jit(solution)/shard_map/ppermute | solution.py:16
  331.0 9.3 %collective-permute-start.4 = (f32[32,32]{1,0:T(8,128)S(1)}, f32[32,32]{1,0:T(8,128)S(1)}, u32[]{:S(2)}, u32[]{:S(2)}) collective-permute-start(f32[32,32]{1,0:T(8,128)S(1)} %fusion.82), channel_id=1, source_target_pairs={{0,1},{1,2},{2,3},{3,4},{4,5},{5,6},{6,7},{7,8},{8,9},{9,10},{10,1... | collective-permute-start | bytes 12296 | tf_op jit(solution)/shard_map/ppermute | solution.py:16
  332.9 9.4 %collective-permute-start.13 = (f32[32]{0:T(128)S(1)}, f32[32]{0:T(128)S(1)}, u32[]{:S(2)}, u32[]{:S(2)}) collective-permute-start(f32[32]{0:T(128)S(1)} %broadcast_select_fusion), channel_id=1, source_target_pairs={{0,1},{1,2},{2,3},{3,4},{4,5},{5,6},{6,7},{7,8},{8,9},{9,10},{10,1... | collective-permute-start | bytes 392 | tf_op jit(solution)/shard_map/ppermute | solution.py:16
  340.4 10.2 %collective-permute-start.5 = (f32[32,32]{1,0:T(8,128)S(1)}, f32[32,32]{1,0:T(8,128)S(1)}, u32[]{:S(2)}, u32[]{:S(2)}) collective-permute-start(f32[32,32]{1,0:T(8,128)S(1)} %convolution_select_fusion.7), channel_id=1, source_target_pairs={{0,2},{1,3},{2,4},{3,5},{4,6},{5,7},{6,8},{7,9},{8,10},{9,11},{10,... | collective-permute-start | bytes 12296 | tf_op jit(solution)/shard_map/ppermute | solution.py:16
  342.5 10.2 %collective-permute-start.14 = (f32[32]{0:T(128)S(1)}, f32[32]{0:T(128)S(1)}, u32[]{:S(2)}, u32[]{:S(2)}) collective-permute-start(f32[32]{0:T(128)S(1)} %fusion.26), channel_id=1, source_target_pairs={{0,2},{1,3},{2,4},{3,5},{4,6},{5,7},{6,8},{7,9},{8,10},{9,11},{10,... | collective-permute-start | bytes 392 | tf_op jit(solution)/shard_map/ppermute | solution.py:16
  350.7 12.0 %collective-permute-start.6 = (f32[32,32]{1,0:T(8,128)S(1)}, f32[32,32]{1,0:T(8,128)S(1)}, u32[]{:S(2)}, u32[]{:S(2)}) collective-permute-start(f32[32,32]{1,0:T(8,128)S(1)} %convolution_select_fusion.6), channel_id=1, source_target_pairs={{0,4},{1,5},{2,6},{3,7},{4,8},{5,9},{6,10},{7,11},{8,12},{9,13},{1... | collective-permute-start | bytes 12296 | tf_op jit(solution)/shard_map/ppermute | solution.py:16
  352.8 12.0 %collective-permute-start.15 = (f32[32]{0:T(128)S(1)}, f32[32]{0:T(128)S(1)}, u32[]{:S(2)}, u32[]{:S(2)}) collective-permute-start(f32[32]{0:T(128)S(1)} %fusion.27), channel_id=1, source_target_pairs={{0,4},{1,5},{2,6},{3,7},{4,8},{5,9},{6,10},{7,11},{8,12},{9,13},{1... | collective-permute-start | bytes 392 | tf_op jit(solution)/shard_map/ppermute | solution.py:16
  362.9 7.2 %collective-permute-start.7 = (f32[32,32]{1,0:T(8,128)S(1)}, f32[32,32]{1,0:T(8,128)S(1)}, u32[]{:S(2)}, u32[]{:S(2)}) collective-permute-start(f32[32,32]{1,0:T(8,128)S(1)} %convolution_select_fusion.5), channel_id=1, source_target_pairs={{0,8},{1,9},{2,10},{3,11},{4,12},{5,13},{6,14},{7,15},{8,16},{9,17... | collective-permute-start | bytes 12296 | tf_op jit(solution)/shard_map/ppermute | solution.py:16
  364.9 7.2 %collective-permute-start.16 = (f32[32]{0:T(128)S(1)}, f32[32]{0:T(128)S(1)}, u32[]{:S(2)}, u32[]{:S(2)}) collective-permute-start(f32[32]{0:T(128)S(1)} %fusion.28), channel_id=1, source_target_pairs={{0,8},{1,9},{2,10},{3,11},{4,12},{5,13},{6,14},{7,15},{8,16},{9,17... | collective-permute-start | bytes 392 | tf_op jit(solution)/shard_map/ppermute | solution.py:16
  370.2 7.7 %collective-permute-start.8 = (f32[32,32]{1,0:T(8,128)S(1)}, f32[32,32]{1,0:T(8,128)S(1)}, u32[]{:S(2)}, u32[]{:S(2)}) collective-permute-start(f32[32,32]{1,0:T(8,128)S(1)} %convolution_select_fusion.4), channel_id=1, source_target_pairs={{0,16},{1,17},{2,18},{3,19},{4,20},{5,21},{6,22},{7,23},{8,24},{9,... | collective-permute-start | bytes 12296 | tf_op jit(solution)/shard_map/ppermute | solution.py:16
  372.2 9.8 %collective-permute-start.17 = (f32[32]{0:T(128)S(1)}, f32[32]{0:T(128)S(1)}, u32[]{:S(2)}, u32[]{:S(2)}) collective-permute-start(f32[32]{0:T(128)S(1)} %fusion.29), channel_id=1, source_target_pairs={{0,16},{1,17},{2,18},{3,19},{4,20},{5,21},{6,22},{7,23},{8,24},{9,... | collective-permute-start | bytes 392 | tf_op jit(solution)/shard_map/ppermute | solution.py:16
  378.0 8.7 %collective-permute-start.9 = (f32[32,32]{1,0:T(8,128)S(1)}, f32[32,32]{1,0:T(8,128)S(1)}, u32[]{:S(2)}, u32[]{:S(2)}) collective-permute-start(f32[32,32]{1,0:T(8,128)S(1)} %convolution_select_fusion.3), channel_id=1, source_target_pairs={{0,32},{1,33},{2,34},{3,35},{4,36},{5,37},{6,38},{7,39},{8,40},{9,... | collective-permute-start | bytes 12296 | tf_op jit(solution)/shard_map/ppermute | solution.py:16
  382.2 7.8 %collective-permute-start.18 = (f32[32]{0:T(128)S(1)}, f32[32]{0:T(128)S(1)}, u32[]{:S(2)}, u32[]{:S(2)}) collective-permute-start(f32[32]{0:T(128)S(1)} %fusion.30), channel_id=1, source_target_pairs={{0,32},{1,33},{2,34},{3,35},{4,36},{5,37},{6,38},{7,39},{8,40},{9,... | collective-permute-start | bytes 392 | tf_op jit(solution)/shard_map/ppermute | solution.py:16
  386.8 5.6 %collective-permute-start.10 = (f32[32,32]{1,0:T(8,128)S(1)}, f32[32,32]{1,0:T(8,128)S(1)}, u32[]{:S(2)}, u32[]{:S(2)}) collective-permute-start(f32[32,32]{1,0:T(8,128)S(1)} %convolution_select_fusion.2), channel_id=1, source_target_pairs={{0,64},{1,65},{2,66},{3,67},{4,68},{5,69},{6,70},{7,71},{8,72},{9,... | collective-permute-start | bytes 12296 | tf_op jit(solution)/shard_map/ppermute | solution.py:16
  390.2 5.4 %collective-permute-start.19 = (f32[32]{0:T(128)S(1)}, f32[32]{0:T(128)S(1)}, u32[]{:S(2)}, u32[]{:S(2)}) collective-permute-start(f32[32]{0:T(128)S(1)} %fusion.31), channel_id=1, source_target_pairs={{0,64},{1,65},{2,66},{3,67},{4,68},{5,69},{6,70},{7,71},{8,72},{9,... | collective-permute-start | bytes 392 | tf_op jit(solution)/shard_map/ppermute | solution.py:16
  392.6 7.1 %collective-permute-start.11 = (f32[32,32]{1,0:T(8,128)S(1)}, f32[32,32]{1,0:T(8,128)S(1)}, u32[]{:S(2)}, u32[]{:S(2)}) collective-permute-start(f32[32,32]{1,0:T(8,128)S(1)} %convolution_select_fusion.1), channel_id=1, source_target_pairs={{0,128},{1,129},{2,130},{3,131},{4,132},{5,133},{6,134},{7,135},{8... | collective-permute-start | bytes 12296 | tf_op jit(solution)/shard_map/ppermute | solution.py:16
  395.7 6.9 %collective-permute-start.20 = (f32[32]{0:T(128)S(1)}, f32[32]{0:T(128)S(1)}, u32[]{:S(2)}, u32[]{:S(2)}) collective-permute-start(f32[32]{0:T(128)S(1)} %fusion.32), channel_id=1, source_target_pairs={{0,128},{1,129},{2,130},{3,131},{4,132},{5,133},{6,134},{7,135},{8... | collective-permute-start | bytes 392 | tf_op jit(solution)/shard_map/ppermute | solution.py:16
  403.5 10.5 %collective-permute-start.21 = (f32[32,1024]{1,0:T(8,128)S(1)}, f32[32,1024]{1,0:T(8,128)S(1)}, u32[]{:S(2)}, u32[]{:S(2)}) collective-permute-start(f32[32,1024]{1,0:T(8,128)S(1)} %get-tuple-element.45), channel_id=1, source_target_pairs={{0,1},{1,2},{2,3},{3,4},{4,5},{5,6},{6,7},{7,8},{8,9},{9,10},{10,1... | collective-permute-start | bytes 393224 | tf_op jit(solution)/shard_map/ppermute | solution.py:27
  405.4 10.4 %collective-permute-start.22 = (f32[32,1024]{1,0:T(8,128)S(1)}, f32[32,1024]{1,0:T(8,128)S(1)}, u32[]{:S(2)}, u32[]{:S(2)}) collective-permute-start(f32[32,1024]{1,0:T(8,128)S(1)} %get-tuple-element.46), channel_id=1, source_target_pairs={{1,0},{2,1},{3,2},{4,3},{5,4},{6,5},{7,6},{8,7},{9,8},{10,9},{11,1... | collective-permute-start | bytes 393224 | tf_op jit(solution)/shard_map/ppermute | solution.py:29
where the time goes:
time: 418 us; the launch traced here: 416 us
  matrix products  176 us (42%)
  other arithmetic  83.9 us (20%)
  starting transfers between devices  56.4 us (13%)
  waiting for transfers between devices  56.4 us (13%)
  loops' own time  30.1 us (7%)
  local copies, waits for them, and re-layouts  12.3 us (3%)
    dot_general x4, matrix products, shards(): projected = jnp.dot(basis_rows, operator, precision=HIGHEST_PRECISION)  101 us
    dot_general x16, matrix products, kernel_block(): jnp.einsum('bd,pd->bp', rows_part, patch_rows, precision=HIGHEST_PRECISION)  61.6 us
    ppermute x18, waiting for transfers between devices, shifted(): return lax.ppermute(value, axis, pairs)  39.4 us
    ppermute x18, starting transfers between devices, shifted(): return lax.ppermute(value, axis, pairs)  39 us
    another operation x1, loops' own time, build_operator(): kernel = lax.map(kernel_block, starts).reshape(total_rows, total_rows)  30.1 us
    mul x1, other arithmetic, build_operator(): return 0.5 * kernel  27.7 us
    reduce_sum x1, other arithmetic, build_operator(): kernel = kernel - jnp.mean(kernel, axis=1, keepdims=True)  14.5 us
    another operation x12, other arithmetic, orthonormal(): cholesky_factor = jnp.linalg.cholesky(covariance)  14.4 us
  transfers between devices with their start and end apart: 23, of which 15 were waited for; matrix products, arithmetic and copies ran while one was open for 3% of the time, Pallas kernels for 0%

commit v1 on v0

v1 whole, which is shorter than its diff:
```python
import functools
import math

import jax
import jax.numpy as jnp
from jax import lax
from jax.experimental import pallas as pl
from jax.experimental.pallas import tpu as pltpu
from jax.sharding import PartitionSpec as P

DIM = 128
EMB = 32
BLOCK = 1024
PATCH = 3 * BLOCK
ITERS = 4
NS_STEPS = 16
CHUNKS = 4
CHUNK = BLOCK // CHUNKS
LOW = 8

F32 = jnp.float32
BF16 = jnp.bfloat16
NT = (((1,), (1,)), ((), ()))
HIGHEST = lax.Precision.HIGHEST
MESH = pl.DeviceIdType.MESH
SCALE = math.sqrt(2.0 * math.log2(math.e) / (0.5 * DIM))


def halves(value):
    high = value.astype(BF16)
    return high, (value - high.astype(F32)).astype(BF16)


def thirds(value):
    high = value.astype(BF16)
    rest = value - high.astype(F32)
    middle = rest.astype(BF16)
    return high, middle, (rest - middle.astype(F32)).astype(BF16)


def prepare(rows, left_ref, right_ref, at):
    count = rows.shape[0]
    scaled = rows * SCALE
    high, low = halves(scaled)
    norms = -0.5 * jnp.sum(scaled * scaled, axis=1, keepdims=True)
    n0, n1, n2 = (part.astype(F32) for part in thirds(norms))
    lane = lax.broadcasted_iota(jnp.int32, (count, DIM), 1)
    tail = jnp.where(
        lane == 0,
        n0,
        jnp.where(lane == 1, n1, jnp.where(lane == 2, n2, jnp.where(lane < 6, 1.0, 0.0))),
    )
    here = pl.ds(at, count)
    left_ref[here, 0:DIM] = high
    left_ref[here, DIM : 2 * DIM] = low
    left_ref[here, 2 * DIM : 3 * DIM] = high
    left_ref[here, 3 * DIM : 4 * DIM] = tail.astype(BF16)
    turned = scaled.T
    high, low = halves(turned)
    norms = -0.5 * jnp.sum(turned * turned, axis=0, keepdims=True)
    n0, n1, n2 = (part.astype(F32) for part in thirds(norms))
    row = lax.broadcasted_iota(jnp.int32, (DIM, count), 0)
    tail = jnp.where(
        row < 3,
        1.0,
        jnp.where(row == 3, n0, jnp.where(row == 4, n1, jnp.where(row == 5, n2, 0.0))),
    )
    right_ref[0:DIM, here] = high
    right_ref[DIM : 2 * DIM, here] = high
    right_ref[2 * DIM : 3 * DIM, here] = low
    right_ref[3 * DIM : 4 * DIM, here] = tail.astype(BF16)


def kernel_tile(left_ref, right_ref, high_ref, low_ref, rows, cols):
    power = jnp.dot(left_ref[rows, :], right_ref[:, cols], preferred_element_type=F32)
    high, low = halves(jnp.exp2(power))
    high_ref[rows, cols] = high
    low_ref[rows, cols] = low


def product_nt(a, b):
    rows = a.shape[0]
    pair_a = jnp.concatenate(halves(a), axis=0)
    pair_b = jnp.concatenate(halves(b), axis=0)
    full = lax.dot_general(pair_a, pair_b, NT, preferred_element_type=F32)
    return full[:rows, :rows] + (full[:rows, rows:] + full[rows:, :rows]) + full[rows:, rows:]


def inverse_factor(gram):
    n = gram.shape[0]
    lane = lax.broadcasted_iota(jnp.int32, (n, 128), 1)
    row = lax.broadcasted_iota(jnp.int32, (n, 128), 0)
    both = jnp.concatenate([gram, jnp.zeros((n, 128 - n), F32)], axis=1)
    both = jnp.where(lane == row + n, 1.0, both)
    for k in range(n - 1):
        pivot = both[k : k + 1, :] / both[k : k + 1, k : k + 1]
        both = jnp.where(row > k, both - both[:, k : k + 1] * pivot, both)
    diagonal = jnp.sum(jnp.where(lane == row, both, 0.0), axis=1, keepdims=True)
    return both[:, n : 2 * n] / jnp.sqrt(diagonal)


def small_times_wide(small, wide):
    s0, s1, s2 = thirds(small)
    w0, w1, w2 = thirds(wide)
    return jnp.dot(
        jnp.concatenate([s0, s1, s0, s2, s1, s0], axis=1),
        jnp.concatenate([w0, w0, w1, w0, w1, w2], axis=0),
        preferred_element_type=F32,
    )


def chained(first, later):
    lane = lax.broadcasted_iota(jnp.int32, first.shape, 1)
    turned = jnp.dot(first[:, :EMB], later, precision=HIGHEST, preferred_element_type=F32)
    return turned + jnp.where(lane == EMB, first, 0.0)


def chain_of(maps):
    while len(maps) > 1:
        joined = [chained(maps[i], maps[i + 1]) for i in range(0, len(maps) - 1, 2)]
        maps = joined + maps[len(maps) - len(maps) % 2 :]
    return maps[0]


def kernel(
    wide_count,
    narrow_count,
    points_ref,
    start_ref,
    out_ref,
    own_ref,
    near_ref,
    left_ref,
    right_ref,
    high_ref,
    low_ref,
    basis_ref,
    image_ref,
    send_ref,
    got_ref,
    ring_ref,
    low_maps_ref,
    high_maps_ref,
    next_map_ref,
    x_send,
    x_recv,
    e_send,
    e_recv,
    m_send,
    m_recv,
    n_send,
    n_recv,
):
    wide = lax.axis_index("wide")
    narrow = lax.axis_index("narrow")
    total = wide_count * narrow_count
    me = wide * narrow_count + narrow
    after = lax.rem(me + 1, total)
    before = lax.rem(me + total - 1, total)
    after_id = (lax.div(after, narrow_count), lax.rem(after, narrow_count))
    before_id = (lax.div(before, narrow_count), lax.rem(before, narrow_count))
    upper = lax.div(wide, LOW)
    lower = lax.rem(wide, LOW)
    uppers = wide_count // LOW

    def along_narrow(step):
        return (wide, lax.rem(narrow + step, narrow_count))

    def along_lower(step):
        return (upper * LOW + lax.rem(lower + step, LOW), narrow)

    def along_upper(step):
        return (lax.rem(upper + step, uppers) * LOW + lower, narrow)

    levels = (
        (along_narrow, narrow_count, narrow, ring_ref),
        (along_lower, LOW, lower, low_maps_ref),
        (along_upper, uppers, upper, high_maps_ref),
    )
    barrier = pltpu.get_barrier_semaphore()
    greeted = 0
    for peer in (after_id, before_id):
        pl.semaphore_signal(barrier, inc=1, device_id=peer, device_id_type=MESH)
        greeted += 1
    for peer_at, count, _, _ in levels:
        for step in range(1, count):
            pl.semaphore_signal(barrier, inc=1, device_id=peer_at(step), device_id_type=MESH)
            greeted += 1
    pl.semaphore_wait(barrier, greeted)

    def remote(source, target, send, recv, peer):
        return pltpu.make_async_remote_copy(
            src_ref=source,
            dst_ref=target,
            send_sem=send,
            recv_sem=recv,
            device_id=peer,
            device_id_type=MESH,
        )

    point_copies = []
    for c in range(CHUNKS):
        rows = points_ref.at[pl.ds(c * CHUNK, CHUNK), :]
        for side, peer in ((0, after_id), (1, before_id)):
            copy = remote(
                rows, near_ref.at[c, side], x_send.at[c, side], x_recv.at[c, side], peer
            )
            copy.start()
            point_copies.append(copy)

    order = [(BLOCK + c * CHUNK, c * CHUNK) for c in range(CHUNKS)]
    for c in range(CHUNKS):
        order.append((c * CHUNK, BLOCK + 2 * c * CHUNK))
        order.append((2 * BLOCK + c * CHUNK, BLOCK + (2 * c + 1) * CHUNK))
    for theirs, mine in order:
        basis_ref[:, mine : mine + CHUNK] = start_ref[:, theirs : theirs + CHUNK]
    for c in range(CHUNKS):
        prepare(points_ref[c * CHUNK : (c + 1) * CHUNK, :], left_ref, right_ref, c * CHUNK)
    kernel_tile(left_ref, right_ref, high_ref, low_ref, slice(0, BLOCK), slice(0, BLOCK))
    for c in range(CHUNKS):
        known = BLOCK + 2 * c * CHUNK
        grown = known + 2 * CHUNK
        for side in (0, 1):
            point_copies[2 * c + side].wait_recv()
            prepare(near_ref[c, side], left_ref, right_ref, known + side * CHUNK)
        kernel_tile(left_ref, right_ref, high_ref, low_ref, slice(0, grown), slice(known, grown))
        kernel_tile(left_ref, right_ref, high_ref, low_ref, slice(known, grown), slice(0, known))

    @pl.loop(0, ITERS)
    def _(_):
        basis = basis_ref[...]
        factor = inverse_factor(product_nt(basis, basis))
        centred = basis - jnp.mean(basis, axis=1, keepdims=True)
        basis_high, basis_low = halves(centred)
        pair = jnp.concatenate([basis_high, basis_low], axis=0)
        for c in range(3):
            cols = slice(c * BLOCK, (c + 1) * BLOCK)
            by_high = jnp.dot(pair, high_ref[:, cols], preferred_element_type=F32)
            by_low = jnp.dot(basis_high, low_ref[:, cols], preferred_element_type=F32)
            image_ref[:, cols] = by_high[:EMB] + (by_high[EMB:] + by_low)
        image = image_ref[...]
        image = 0.5 * (image - jnp.mean(image, axis=1, keepdims=True))
        basis_ref[...] = small_times_wide(factor, image)

    image = basis_ref[...]
    size = jnp.sum(image * image, axis=1, keepdims=True) + 1e-06
    embedded = image / jnp.sqrt(jnp.sqrt(size))
    send_ref[0] = embedded[:, :BLOCK]
    for c in range(CHUNKS):
        at = BLOCK + 2 * c * CHUNK
        send_ref[2, :, c * CHUNK : (c + 1) * CHUNK] = embedded[:, at : at + CHUNK]
        send_ref[1, :, c * CHUNK : (c + 1) * CHUNK] = embedded[:, at + CHUNK : at + 2 * CHUNK]
    block_copies = []
    for part, peer in ((0, after_id), (1, after_id), (2, before_id)):
        copy = remote(send_ref.at[part], got_ref.at[part], e_send.at[part], e_recv.at[part], peer)
        copy.start()
        block_copies.append(copy)
    block_copies[0].wait_recv()
    block_copies[1].wait_recv()

    source = jnp.concatenate([send_ref[2], send_ref[0]], axis=1)
    target = jnp.concatenate([got_ref[0], got_ref[1]], axis=1)
    source_mean = jnp.mean(source, axis=1, keepdims=True)
    target_mean = jnp.mean(target, axis=1, keepdims=True)
    covariance = product_nt(target - target_mean, source - source_mean)
    turn = covariance / jnp.sqrt(jnp.sum(covariance * covariance) + 1e-06)

    def newton_schulz(_, turn):
        square = lax.dot_general(
            turn, turn, NT, precision=HIGHEST, preferred_element_type=F32
        )
        return 1.5 * turn - 0.5 * jnp.dot(
            square, turn, precision=HIGHEST, preferred_element_type=F32
        )

    turn = lax.fori_loop(0, NS_STEPS, newton_schulz, turn)
    lane = lax.broadcasted_iota(jnp.int32, (EMB, 128), 1)
    row = lax.broadcasted_iota(jnp.int32, (EMB, 128), 0)
    moved = jnp.dot(
        turn,
        jnp.where(lane == EMB, source_mean, 0.0),
        precision=HIGHEST,
        preferred_element_type=F32,
    )
    own_map = jnp.concatenate([turn, jnp.zeros((EMB, 128 - EMB), F32)], axis=1)
    own_map = own_map + (jnp.where(lane == EMB, target_mean, 0.0) - moved)
    unit = jnp.where(lane == row, 1.0, 0.0)

    own_ref[...] = own_map
    next_copy = remote(own_ref, next_map_ref, n_send, n_recv, before_id)
    next_copy.start()
    level_copies = []
    passed = own_map
    prefix = None
    slot = 0
    for level, (peer_at, count, place, maps_ref) in enumerate(levels):
        maps_ref[place] = passed
        for step in range(1, count):
            copy = remote(
                maps_ref.at[place],
                maps_ref.at[place],
                m_send.at[slot + step - 1],
                m_recv.at[slot + step - 1],
                peer_at(step),
            )
            copy.start()
            level_copies.append(copy)
        for step in range(1, count):
            origin = lax.rem(place + count - step, count)
            remote(
                maps_ref.at[origin],
                maps_ref.at[origin],
                m_send.at[slot + step - 1],
                m_recv.at[slot + step - 1],
                peer_at(step),
            ).wait_recv()
        slot += count - 1
        maps = [maps_ref[j] for j in range(count)]
        if level + 1 < len(levels):
            passed = chain_of(maps)
        masked = []
        for j in range(count - 1):
            earlier = jnp.where(j < place, 1.0, 0.0).astype(F32)
            masked.append(earlier * maps[j] + (1.0 - earlier) * unit)
        earlier_maps = chain_of(masked)
        prefix = earlier_maps if prefix is None else chained(earlier_maps, prefix)

    has_prev = jnp.where(me > 0, 1.0, 0.0).astype(F32)
    has_next = jnp.where(me < total - 1, 1.0, 0.0).astype(F32)
    composite = chained(prefix, own_map)
    next_copy.wait_recv()
    following = chained(composite, next_map_ref[...])
    share = 1.0 / (1.0 + has_prev + has_next)
    maps = (composite * share, prefix * (has_prev * share), following * (has_next * share))
    offset = (maps[0] + maps[1] + maps[2])[:, EMB : EMB + 1]
    block_copies[2].wait_recv()
    columns = jnp.concatenate([send_ref[0], got_ref[1], got_ref[2]], axis=0)
    columns_high, columns_low = halves(columns)
    joined = jnp.concatenate([m[:, :EMB] for m in maps], axis=1)
    joined_high, joined_low = halves(joined)
    out_ref[...] = (
        jnp.dot(
            jnp.concatenate([joined_high, joined_low, joined_high], axis=1),
            jnp.concatenate([columns_high, columns_high, columns_low], axis=0),
            preferred_element_type=F32,
        )
        + offset
    )
    for copy in point_copies + block_copies + level_copies + [next_copy]:
        copy.wait_send()


def shards(wide_count, narrow_count, points, start_basis):
    messages = (narrow_count - 1) + (LOW - 1) + (wide_count // LOW - 1)
    in_vmem = pl.BlockSpec(memory_space=pltpu.VMEM)
    return pl.pallas_call(
        functools.partial(kernel, wide_count, narrow_count),
        out_shape=jax.ShapeDtypeStruct((EMB, BLOCK), F32),
        in_specs=[in_vmem, in_vmem],
        out_specs=in_vmem,
        scratch_shapes=[
            pltpu.VMEM((EMB, 128), F32),
            pltpu.VMEM((CHUNKS, 2, CHUNK, DIM), F32),
            pltpu.VMEM((PATCH, 4 * DIM), BF16),
            pltpu.VMEM((4 * DIM, PATCH), BF16),
            pltpu.VMEM((PATCH, PATCH), BF16),
            pltpu.VMEM((PATCH, PATCH), BF16),
            pltpu.VMEM((EMB, PATCH), F32),
            pltpu.VMEM((EMB, PATCH), F32),
            pltpu.VMEM((3, EMB, BLOCK), F32),
            pltpu.VMEM((3, EMB, BLOCK), F32),
            pltpu.VMEM((narrow_count, EMB, 128), F32),
            pltpu.VMEM((LOW, EMB, 128), F32),
            pltpu.VMEM((wide_count // LOW, EMB, 128), F32),
            pltpu.VMEM((EMB, 128), F32),
            pltpu.SemaphoreType.DMA((CHUNKS, 2)),
            pltpu.SemaphoreType.DMA((CHUNKS, 2)),
            pltpu.SemaphoreType.DMA((3,)),
            pltpu.SemaphoreType.DMA((3,)),
            pltpu.SemaphoreType.DMA((messages,)),
            pltpu.SemaphoreType.DMA((messages,)),
            pltpu.SemaphoreType.DMA,
            pltpu.SemaphoreType.DMA,
        ],
        compiler_params=pltpu.CompilerParams(
            collective_id=0, has_side_effects=True, vmem_limit_bytes=61 * 1024 * 1024
        ),
    )(points, start_basis)


def solution(mesh):
    placed = (P(("wide", "narrow"), None), P(None, ("wide", "narrow")))
    return jax.shard_map(
        functools.partial(shards, mesh.shape["wide"], mesh.shape["narrow"]),
        mesh=mesh,
        in_specs=placed,
        out_specs=P(None, ("wide", "narrow")),
        check_vma=False,
    )
```

time: 418 us -> 86.2 us (0.21)
  the two profiles are of different devices: /device:TPU:16 before, /device:TPU:1 now
where the time goes in v1:
time: 86.2 us; the launch traced here: 86.1 us
  Pallas kernels  84.6 us (98%)
  local copies, waits for them, and re-layouts  1.57 us (2%)
    pallas_call x1, Pallas kernels, shards(): pl.pallas_call(functools.partial(kernel, wide_count, narrow_count), out_s...  84.6 us

profile of v1, /device:TPU:1, one launch (start us, length us, event | category | flops | bytes accessed | tf_op | source)
XLA Modules:
  0.0 86.1 jit_solution(15253719042637802448)
XLA Ops:
  0.0 84.6 %shard_map.28 = f32[32,1024]{1,0:T(8,128)} custom-call(f32[1024,128]{1,0:T(8,128)} %points_ref.1, f32[32,3072]{1,0:T(8,128)} %start_ref.1), custom_call_target="tpu_custom_call" | custom-call | tf_op jit(solution)/shard_map/pallas_call | solution.py:356
  84.6 1.6 %copy.4 = f32[32,1024]{1,0:T(8,128)} copy(f32[32,1024]{1,0:T(8,128)} %shard_map.28) | data formatting | bytes 262144

commit v2 on v1

--- a/solution.py
+++ b/solution.py
@@ -16,6 +16,7 @@
 NS_STEPS = 16
 CHUNKS = 4
 CHUNK = BLOCK // CHUNKS
+MAP = 64
 LOW = 8
 
 F32 = jnp.float32
@@ -100,19 +101,34 @@
 
 
 def small_times_wide(small, wide):
-    s0, s1, s2 = thirds(small)
-    w0, w1, w2 = thirds(wide)
+    small_high, small_low = halves(small)
+    wide_high, wide_low = halves(wide)
     return jnp.dot(
-        jnp.concatenate([s0, s1, s0, s2, s1, s0], axis=1),
-        jnp.concatenate([w0, w0, w1, w0, w1, w2], axis=0),
+        jnp.concatenate([small_high, small_low, small_high], axis=1),
+        jnp.concatenate([wide_high, wide_high, wide_low], axis=0),
         preferred_element_type=F32,
     )
 
 
 def chained(first, later):
     lane = lax.broadcasted_iota(jnp.int32, first.shape, 1)
-    turned = jnp.dot(first[:, :EMB], later, precision=HIGHEST, preferred_element_type=F32)
-    return turned + jnp.where(lane == EMB, first, 0.0)
+    first_high, first_low = halves(first[:, :EMB])
+    later_high, later_low = halves(later)
+    by_high = jnp.dot(
+        jnp.concatenate([first_high, first_low], axis=0), later_high, preferred_element_type=F32
+    )
+    by_low = jnp.dot(first_high, later_low, preferred_element_type=F32)
+    moved = by_high[:EMB] + (by_high[EMB:] + by_low)
+    return moved + jnp.where(lane == EMB, first, 0.0)
+
+
+def packed(value):
+    half = EMB // 2
+    return jnp.concatenate([value[:half], value[half:]], axis=1)
+
+
+def unpacked(value):
+    return jnp.concatenate([value[:, :MAP], value[:, MAP:]], axis=0)
 
 
 def chain_of(maps):
@@ -136,6 +152,9 @@
     low_ref,
     basis_ref,
     image_ref,
+    columns_ref,
+    stats_ref,
+    near_stats_ref,
     send_ref,
     got_ref,
     ring_ref,
@@ -146,6 +165,8 @@
     x_recv,
     e_send,
     e_recv,
+    s_send,
+    s_recv,
     m_send,
     m_recv,
     n_send,
@@ -200,69 +221,86 @@
 
     point_copies = []
     for c in range(CHUNKS):
-        rows = points_ref.at[pl.ds(c * CHUNK, CHUNK), :]
         for side, peer in ((0, after_id), (1, before_id)):
+            at = BLOCK - (c + 1) * CHUNK if side == 0 else c * CHUNK
+            rows = points_ref.at[pl.ds(at, CHUNK), :]
             copy = remote(
                 rows, near_ref.at[c, side], x_send.at[c, side], x_recv.at[c, side], peer
             )
             copy.start()
             point_copies.append(copy)
 
-    order = [(BLOCK + c * CHUNK, c * CHUNK) for c in range(CHUNKS)]
+    basis_ref[...] = start_ref[...]
     for c in range(CHUNKS):
-        order.append((c * CHUNK, BLOCK + 2 * c * CHUNK))
-        order.append((2 * BLOCK + c * CHUNK, BLOCK + (2 * c + 1) * CHUNK))
-    for theirs, mine in order:
-        basis_ref[:, mine : mine + CHUNK] = start_ref[:, theirs : theirs + CHUNK]
+        at = BLOCK + c * CHUNK
+        prepare(points_ref[c * CHUNK : (c + 1) * CHUNK, :], left_ref, right_ref, at)
+    tile = functools.partial(kernel_tile, left_ref, right_ref, high_ref, low_ref)
+    tile(slice(BLOCK, 2 * BLOCK), slice(BLOCK, 2 * BLOCK))
     for c in range(CHUNKS):
-        prepare(points_ref[c * CHUNK : (c + 1) * CHUNK, :], left_ref, right_ref, c * CHUNK)
-    kernel_tile(left_ref, right_ref, high_ref, low_ref, slice(0, BLOCK), slice(0, BLOCK))
-    for c in range(CHUNKS):
-        known = BLOCK + 2 * c * CHUNK
-        grown = known + 2 * CHUNK
+        first, last = BLOCK - c * CHUNK, 2 * BLOCK + c * CHUNK
+        known, grown = slice(first, last), slice(first - CHUNK, last + CHUNK)
+        sides = (slice(first - CHUNK, first), slice(last, last + CHUNK))
         for side in (0, 1):
             point_copies[2 * c + side].wait_recv()
-            prepare(near_ref[c, side], left_ref, right_ref, known + side * CHUNK)
-        kernel_tile(left_ref, right_ref, high_ref, low_ref, slice(0, grown), slice(known, grown))
-        kernel_tile(left_ref, right_ref, high_ref, low_ref, slice(known, grown), slice(0, known))
-
-    @pl.loop(0, ITERS)
+            prepare(near_ref[c, side], left_ref, right_ref, sides[side].start)
+        for side in (0, 1):
+            tile(grown, sides[side])
+            tile(sides[side], known)
+
+    def factor_and_pair():
+        basis = basis_ref[...]
+        factor = 0.5 * inverse_factor(product_nt(basis, basis))
+        high, low = halves(basis - jnp.mean(basis, axis=1, keepdims=True))
+        return factor, jnp.concatenate([high, low], axis=0)
+
+    def product(pair, part):
+        cols = slice(part * BLOCK, (part + 1) * BLOCK)
+        by_high = jnp.dot(pair, high_ref[:, cols], preferred_element_type=F32)
+        by_low = jnp.dot(pair[:EMB], low_ref[:, cols], preferred_element_type=F32)
+        return by_high[:EMB] + (by_high[EMB:] + by_low)
+
+    @pl.loop(0, ITERS - 1)
     def _(_):
-        basis = basis_ref[...]
-        factor = inverse_factor(product_nt(basis, basis))
-        centred = basis - jnp.mean(basis, axis=1, keepdims=True)
-        basis_high, basis_low = halves(centred)
-        pair = jnp.concatenate([basis_high, basis_low], axis=0)
-        for c in range(3):
-            cols = slice(c * BLOCK, (c + 1) * BLOCK)
-            by_high = jnp.dot(pair, high_ref[:, cols], preferred_element_type=F32)
-            by_low = jnp.dot(basis_high, low_ref[:, cols], preferred_element_type=F32)
-            image_ref[:, cols] = by_high[:EMB] + (by_high[EMB:] + by_low)
+        factor, pair = factor_and_pair()
+        for part in range(3):
+            image_ref[:, part * BLOCK : (part + 1) * BLOCK] = product(pair, part)
         image = image_ref[...]
-        image = 0.5 * (image - jnp.mean(image, axis=1, keepdims=True))
+        image = image - jnp.mean(image, axis=1, keepdims=True)
         basis_ref[...] = small_times_wide(factor, image)
 
-    image = basis_ref[...]
-    size = jnp.sum(image * image, axis=1, keepdims=True) + 1e-06
-    embedded = image / jnp.sqrt(jnp.sqrt(size))
-    send_ref[0] = embedded[:, :BLOCK]
-    for c in range(CHUNKS):
-        at = BLOCK + 2 * c * CHUNK
-        send_ref[2, :, c * CHUNK : (c + 1) * CHUNK] = embedded[:, at : at + CHUNK]
-        send_ref[1, :, c * CHUNK : (c + 1) * CHUNK] = embedded[:, at + CHUNK : at + 2 * CHUNK]
+    factor, pair = factor_and_pair()
     block_copies = []
-    for part, peer in ((0, after_id), (1, after_id), (2, before_id)):
+    for part, peer in ((1, after_id), (2, after_id), (0, before_id)):
+        send_ref[part] = small_times_wide(factor, product(pair, part))
         copy = remote(send_ref.at[part], got_ref.at[part], e_send.at[part], e_recv.at[part], peer)
+        copy.start()
+        block_copies.append(copy)
+    image = jnp.concatenate([send_ref[0], send_ref[1], send_ref[2]], axis=1)
+    image_mean = jnp.mean(image, axis=1, keepdims=True)
+    centred = image - image_mean
+    size = jnp.sum(centred * centred, axis=1, keepdims=True) + 1e-06
+    image_scale = 1.0 / jnp.sqrt(jnp.sqrt(size))
+    lane = lax.broadcasted_iota(jnp.int32, (EMB, 128), 1)
+    stats_ref[...] = jnp.where(lane == 0, image_mean, image_scale)
+    for side, peer in ((0, after_id), (1, before_id)):
+        copy = remote(
+            stats_ref, near_stats_ref.at[side], s_send.at[side], s_recv.at[side], peer
+        )
         copy.start()
         block_copies.append(copy)
     block_copies[0].wait_recv()
     block_copies[1].wait_recv()
 
-    source = jnp.concatenate([send_ref[2], send_ref[0]], axis=1)
-    target = jnp.concatenate([got_ref[0], got_ref[1]], axis=1)
+    source = jnp.concatenate([send_ref[0], send_ref[1]], axis=1)
+    target = jnp.concatenate([got_ref[1], got_ref[2]], axis=1)
     source_mean = jnp.mean(source, axis=1, keepdims=True)
     target_mean = jnp.mean(target, axis=1, keepdims=True)
-    covariance = product_nt(target - target_mean, source - source_mean)
+    covariance = product_nt(target - target_mean, (source - source_mean) * image_scale)
+    block_copies[3].wait_recv()
+    prev_mean, prev_scale = near_stats_ref[0, :, 0:1], near_stats_ref[0, :, 1:2]
+    source_mean = (source_mean - image_mean) * image_scale
+    target_mean = (target_mean - prev_mean) * prev_scale
+    covariance = covariance * prev_scale
     turn = covariance / jnp.sqrt(jnp.sum(covariance * covariance) + 1e-06)
 
     def newton_schulz(_, turn):
@@ -274,27 +312,26 @@
         )
 
     turn = lax.fori_loop(0, NS_STEPS, newton_schulz, turn)
-    lane = lax.broadcasted_iota(jnp.int32, (EMB, 128), 1)
-    row = lax.broadcasted_iota(jnp.int32, (EMB, 128), 0)
+    lane = lax.broadcasted_iota(jnp.int32, (EMB, MAP), 1)
+    row = lax.broadcasted_iota(jnp.int32, (EMB, MAP), 0)
     moved = jnp.dot(
         turn,
         jnp.where(lane == EMB, source_mean, 0.0),
         precision=HIGHEST,
         preferred_element_type=F32,
     )
-    own_map = jnp.concatenate([turn, jnp.zeros((EMB, 128 - EMB), F32)], axis=1)
+    own_map = jnp.concatenate([turn, jnp.zeros((EMB, MAP - EMB), F32)], axis=1)
     own_map = own_map + (jnp.where(lane == EMB, target_mean, 0.0) - moved)
     unit = jnp.where(lane == row, 1.0, 0.0)
 
-    own_ref[...] = own_map
+    own_ref[...] = packed(own_map)
     next_copy = remote(own_ref, next_map_ref, n_send, n_recv, before_id)
-    next_copy.start()
     level_copies = []
     passed = own_map
     prefix = None
     slot = 0
     for level, (peer_at, count, place, maps_ref) in enumerate(levels):
-        maps_ref[place] = passed
+        maps_ref[place] = packed(passed)
         for step in range(1, count):
             copy = remote(
                 maps_ref.at[place],
@@ -305,6 +342,21 @@
             )
             copy.start()
             level_copies.append(copy)
+        if level == 0:
+            next_copy.start()
+            block_copies[2].wait_recv()
+            block_copies[4].wait_recv()
+            next_mean, next_scale = near_stats_ref[1, :, 0:1], near_stats_ref[1, :, 1:2]
+            columns = jnp.concatenate(
+                [
+                    (send_ref[1] - image_mean) * image_scale,
+                    (got_ref[2] - prev_mean) * prev_scale,
+                    (got_ref[0] - next_mean) * next_scale,
+                ],
+                axis=0,
+            )
+            columns_high, columns_low = halves(columns)
+            columns_ref[...] = jnp.concatenate([columns_high, columns_high, columns_low], axis=0)
         for step in range(1, count):
             origin = lax.rem(place + count - step, count)
             remote(
@@ -315,7 +367,7 @@
                 peer_at(step),
             ).wait_recv()
         slot += count - 1
-        maps = [maps_ref[j] for j in range(count)]
+        maps = [unpacked(maps_ref[j]) for j in range(count)]
         if level + 1 < len(levels):
             passed = chain_of(maps)
         masked = []
@@ -329,19 +381,15 @@
     has_next = jnp.where(me < total - 1, 1.0, 0.0).astype(F32)
     composite = chained(prefix, own_map)
     next_copy.wait_recv()
-    following = chained(composite, next_map_ref[...])
+    following = chained(composite, unpacked(next_map_ref[...]))
     share = 1.0 / (1.0 + has_prev + has_next)
     maps = (composite * share, prefix * (has_prev * share), following * (has_next * share))
     offset = (maps[0] + maps[1] + maps[2])[:, EMB : EMB + 1]
-    block_copies[2].wait_recv()
-    columns = jnp.concatenate([send_ref[0], got_ref[1], got_ref[2]], axis=0)
-    columns_high, columns_low = halves(columns)
-    joined = jnp.concatenate([m[:, :EMB] for m in maps], axis=1)
-    joined_high, joined_low = halves(joined)
+    joined_high, joined_low = halves(jnp.concatenate([m[:, :EMB] for m in maps], axis=1))
     out_ref[...] = (
         jnp.dot(
             jnp.concatenate([joined_high, joined_low, joined_high], axis=1),
-            jnp.concatenate([columns_high, columns_high, columns_low], axis=0),
+            columns_ref[...],
             preferred_element_type=F32,
         )
         + offset
@@ -359,7 +407,7 @@
         in_specs=[in_vmem, in_vmem],
         out_specs=in_vmem,
         scratch_shapes=[
-            pltpu.VMEM((EMB, 128), F32),
+            pltpu.VMEM((EMB // 2, 2 * MAP), F32),
             pltpu.VMEM((CHUNKS, 2, CHUNK, DIM), F32),
             pltpu.VMEM((PATCH, 4 * DIM), BF16),
             pltpu.VMEM((4 * DIM, PATCH), BF16),
@@ -367,16 +415,21 @@
             pltpu.VMEM((PATCH, PATCH), BF16),
             pltpu.VMEM((EMB, PATCH), F32),
             pltpu.VMEM((EMB, PATCH), F32),
+            pltpu.VMEM((9 * EMB, BLOCK), BF16),
+            pltpu.VMEM((EMB, 128), F32),
+            pltpu.VMEM((2, EMB, 128), F32),
             pltpu.VMEM((3, EMB, BLOCK), F32),
             pltpu.VMEM((3, EMB, BLOCK), F32),
-            pltpu.VMEM((narrow_count, EMB, 128), F32),
-            pltpu.VMEM((LOW, EMB, 128), F32),
-            pltpu.VMEM((wide_count // LOW, EMB, 128), F32),
-            pltpu.VMEM((EMB, 128), F32),
+            pltpu.VMEM((narrow_count, EMB // 2, 2 * MAP), F32),
+            pltpu.VMEM((LOW, EMB // 2, 2 * MAP), F32),
+            pltpu.VMEM((wide_count // LOW, EMB // 2, 2 * MAP), F32),
+            pltpu.VMEM((EMB // 2, 2 * MAP), F32),
             pltpu.SemaphoreType.DMA((CHUNKS, 2)),
             pltpu.SemaphoreType.DMA((CHUNKS, 2)),
             pltpu.SemaphoreType.DMA((3,)),
             pltpu.SemaphoreType.DMA((3,)),
+            pltpu.SemaphoreType.DMA((2,)),
+            pltpu.SemaphoreType.DMA((2,)),
             pltpu.SemaphoreType.DMA((messages,)),
             pltpu.SemaphoreType.DMA((messages,)),
             pltpu.SemaphoreType.DMA,

time: 86.2 us -> 81.5 us (0.945)
  Pallas kernels: 84.6 us -> 79.8 us
    pallas_call x1, Pallas kernels: 84.6 us -> 79.8 us  [shards(): pl.pallas_call(functools.partial(kernel, wide_count, narrow_count), out_s...]
where the time goes in v2:
time: 81.5 us; the launch traced here: 81.4 us
  Pallas kernels  79.8 us (98%)
  local copies, waits for them, and re-layouts  1.57 us (2%)
    pallas_call x1, Pallas kernels, shards(): pl.pallas_call(functools.partial(kernel, wide_count, narrow_count), out_s...  79.8 us

profile of v2, /device:TPU:1, one launch (start us, length us, event | category | flops | bytes accessed | tf_op | source)
XLA Modules:
  0.0 81.4 jit_solution(16733137195165072127)
XLA Ops:
  0.0 79.8 %shard_map.28 = f32[32,1024]{1,0:T(8,128)} custom-call(f32[1024,128]{1,0:T(8,128)} %points_ref.1, f32[32,3072]{1,0:T(8,128)} %start_ref.1), custom_call_target="tpu_custom_call" | custom-call | tf_op jit(solution)/shard_map/pallas_call | solution.py:404
  79.8 1.6 %copy.4 = f32[32,1024]{1,0:T(8,128)} copy(f32[32,1024]{1,0:T(8,128)} %shard_map.28) | data formatting | bytes 262144

commit v3 on v2

--- a/solution.py
+++ b/solution.py
@@ -271,36 +271,51 @@
     factor, pair = factor_and_pair()
     block_copies = []
     for part, peer in ((1, after_id), (2, after_id), (0, before_id)):
-        send_ref[part] = small_times_wide(factor, product(pair, part))
+        send_ref[part] = product(pair, part)
         copy = remote(send_ref.at[part], got_ref.at[part], e_send.at[part], e_recv.at[part], peer)
         copy.start()
         block_copies.append(copy)
-    image = jnp.concatenate([send_ref[0], send_ref[1], send_ref[2]], axis=1)
-    image_mean = jnp.mean(image, axis=1, keepdims=True)
-    centred = image - image_mean
-    size = jnp.sum(centred * centred, axis=1, keepdims=True) + 1e-06
-    image_scale = 1.0 / jnp.sqrt(jnp.sqrt(size))
-    lane = lax.broadcasted_iota(jnp.int32, (EMB, 128), 1)
-    stats_ref[...] = jnp.where(lane == 0, image_mean, image_scale)
+    raw = jnp.concatenate([send_ref[0], send_ref[1], send_ref[2]], axis=1)
+    raw_mean = jnp.mean(raw, axis=1, keepdims=True)
+    image = small_times_wide(factor, raw - raw_mean)
+    image = image - jnp.mean(image, axis=1, keepdims=True)
+    size = jnp.sum(image * image, axis=1, keepdims=True) + 1e-06
+    scale = 1.0 / jnp.sqrt(jnp.sqrt(size))
+    to_embedded = jnp.concatenate([factor * scale, jnp.zeros((EMB, MAP - EMB), F32)], axis=1)
+    lane = lax.broadcasted_iota(jnp.int32, (EMB, MAP), 1)
+    row = lax.broadcasted_iota(jnp.int32, (EMB, MAP), 0)
+    stats_ref[...] = packed(jnp.where(lane == EMB, raw_mean, to_embedded))
     for side, peer in ((0, after_id), (1, before_id)):
         copy = remote(
             stats_ref, near_stats_ref.at[side], s_send.at[side], s_recv.at[side], peer
         )
         copy.start()
         block_copies.append(copy)
+    image_ref[:, : 2 * BLOCK] = image[:, : 2 * BLOCK] * scale
+
+    source = image_ref[:, : 2 * BLOCK]
+    source_mean = jnp.mean(source, axis=1, keepdims=True)
+    source = source - source_mean
     block_copies[0].wait_recv()
+    target = got_ref[1]
+    covariance = product_nt(target, source[:, :BLOCK])
+    target_mean = jnp.sum(target, axis=1, keepdims=True)
     block_copies[1].wait_recv()
-
-    source = jnp.concatenate([send_ref[0], send_ref[1]], axis=1)
-    target = jnp.concatenate([got_ref[1], got_ref[2]], axis=1)
-    source_mean = jnp.mean(source, axis=1, keepdims=True)
-    target_mean = jnp.mean(target, axis=1, keepdims=True)
-    covariance = product_nt(target - target_mean, (source - source_mean) * image_scale)
+    target = got_ref[2]
+    covariance = covariance + product_nt(target, source[:, BLOCK:])
+    target_mean = (target_mean + jnp.sum(target, axis=1, keepdims=True)) / (2.0 * BLOCK)
     block_copies[3].wait_recv()
-    prev_mean, prev_scale = near_stats_ref[0, :, 0:1], near_stats_ref[0, :, 1:2]
-    source_mean = (source_mean - image_mean) * image_scale
-    target_mean = (target_mean - prev_mean) * prev_scale
-    covariance = covariance * prev_scale
+    prev_stats = unpacked(near_stats_ref[0])
+    prev_mean = prev_stats[:, EMB : EMB + 1]
+    covariance = jnp.concatenate([covariance, jnp.zeros((EMB, MAP - EMB), F32)], axis=1)
+    covariance = jnp.dot(
+        prev_stats[:, :EMB],
+        jnp.where(lane == EMB, target_mean - prev_mean, covariance),
+        precision=HIGHEST,
+        preferred_element_type=F32,
+    )
+    target_mean = covariance[:, EMB : EMB + 1]
+    covariance = covariance[:, :EMB]
     turn = covariance / jnp.sqrt(jnp.sum(covariance * covariance) + 1e-06)
 
     def newton_schulz(_, turn):
@@ -312,8 +327,6 @@
         )
 
     turn = lax.fori_loop(0, NS_STEPS, newton_schulz, turn)
-    lane = lax.broadcasted_iota(jnp.int32, (EMB, MAP), 1)
-    row = lax.broadcasted_iota(jnp.int32, (EMB, MAP), 0)
     moved = jnp.dot(
         turn,
         jnp.where(lane == EMB, source_mean, 0.0),
@@ -323,77 +336,85 @@
     own_map = jnp.concatenate([turn, jnp.zeros((EMB, MAP - EMB), F32)], axis=1)
     own_map = own_map + (jnp.where(lane == EMB, target_mean, 0.0) - moved)
     unit = jnp.where(lane == row, 1.0, 0.0)
-
-    own_ref[...] = packed(own_map)
-    next_copy = remote(own_ref, next_map_ref, n_send, n_recv, before_id)
-    level_copies = []
-    passed = own_map
-    prefix = None
-    slot = 0
-    for level, (peer_at, count, place, maps_ref) in enumerate(levels):
-        maps_ref[place] = packed(passed)
+    has_prev = jnp.where(me > 0, 1.0, 0.0).astype(F32)
+    has_next = jnp.where(me < total - 1, 1.0, 0.0).astype(F32)
+    share = 1.0 / (1.0 + has_prev + has_next)
+
+    def gather_start(level, value):
+        peer_at, count, place, maps_ref = levels[level]
+        maps_ref[place] = packed(value)
+        copies = []
         for step in range(1, count):
             copy = remote(
                 maps_ref.at[place],
                 maps_ref.at[place],
-                m_send.at[slot + step - 1],
-                m_recv.at[slot + step - 1],
+                m_send.at[slots[level] + step - 1],
+                m_recv.at[slots[level] + step - 1],
                 peer_at(step),
             )
             copy.start()
-            level_copies.append(copy)
-        if level == 0:
-            next_copy.start()
-            block_copies[2].wait_recv()
-            block_copies[4].wait_recv()
-            next_mean, next_scale = near_stats_ref[1, :, 0:1], near_stats_ref[1, :, 1:2]
-            columns = jnp.concatenate(
-                [
-                    (send_ref[1] - image_mean) * image_scale,
-                    (got_ref[2] - prev_mean) * prev_scale,
-                    (got_ref[0] - next_mean) * next_scale,
-                ],
-                axis=0,
-            )
-            columns_high, columns_low = halves(columns)
-            columns_ref[...] = jnp.concatenate([columns_high, columns_high, columns_low], axis=0)
+            copies.append(copy)
+        return copies
+
+    def gather_end(level):
+        peer_at, count, place, maps_ref = levels[level]
         for step in range(1, count):
             origin = lax.rem(place + count - step, count)
             remote(
                 maps_ref.at[origin],
                 maps_ref.at[origin],
-                m_send.at[slot + step - 1],
-                m_recv.at[slot + step - 1],
+                m_send.at[slots[level] + step - 1],
+                m_recv.at[slots[level] + step - 1],
                 peer_at(step),
             ).wait_recv()
-        slot += count - 1
         maps = [unpacked(maps_ref[j]) for j in range(count)]
-        if level + 1 < len(levels):
-            passed = chain_of(maps)
         masked = []
         for j in range(count - 1):
             earlier = jnp.where(j < place, 1.0, 0.0).astype(F32)
             masked.append(earlier * maps[j] + (1.0 - earlier) * unit)
-        earlier_maps = chain_of(masked)
-        prefix = earlier_maps if prefix is None else chained(earlier_maps, prefix)
-
-    has_prev = jnp.where(me > 0, 1.0, 0.0).astype(F32)
-    has_next = jnp.where(me < total - 1, 1.0, 0.0).astype(F32)
-    composite = chained(prefix, own_map)
+        return maps, masked
+
+    slots = (0, narrow_count - 1, narrow_count + LOW - 2)
+    own_ref[...] = packed(own_map)
+    level_copies = gather_start(0, own_map)
+    next_copy = remote(own_ref, next_map_ref, n_send, n_recv, before_id)
+    next_copy.start()
+    block_copies[2].wait_recv()
+    block_copies[4].wait_recv()
+    next_stats = unpacked(near_stats_ref[1])
+    columns = jnp.concatenate(
+        [
+            image_ref[:, BLOCK : 2 * BLOCK],
+            small_times_wide(prev_stats[:, :EMB], got_ref[2] - prev_mean),
+            small_times_wide(next_stats[:, :EMB], got_ref[0] - next_stats[:, EMB : EMB + 1]),
+        ],
+        axis=0,
+    )
+    columns_high, columns_low = halves(columns)
+    columns_ref[...] = jnp.concatenate([columns_high, columns_high, columns_low], axis=0)
+    maps, masked = gather_end(0)
+    level_copies += gather_start(1, chain_of(maps))
+    prefix = chain_of(masked)
     next_copy.wait_recv()
-    following = chained(composite, unpacked(next_map_ref[...]))
-    share = 1.0 / (1.0 + has_prev + has_next)
-    maps = (composite * share, prefix * (has_prev * share), following * (has_next * share))
-    offset = (maps[0] + maps[1] + maps[2])[:, EMB : EMB + 1]
+    own_and_next = chained(own_map, unpacked(next_map_ref[...]))
+    maps, masked = gather_end(1)
+    level_copies += gather_start(2, chain_of(maps))
+    prefix = chained(chain_of(masked), prefix)
+    maps = (
+        chained(prefix, own_map) * share,
+        prefix * (has_prev * share),
+        chained(prefix, own_and_next) * (has_next * share),
+    )
     joined_high, joined_low = halves(jnp.concatenate([m[:, :EMB] for m in maps], axis=1))
-    out_ref[...] = (
-        jnp.dot(
-            jnp.concatenate([joined_high, joined_low, joined_high], axis=1),
-            columns_ref[...],
-            preferred_element_type=F32,
-        )
-        + offset
-    )
+    aligned = jnp.dot(
+        jnp.concatenate([joined_high, joined_low, joined_high], axis=1),
+        columns_ref[...],
+        preferred_element_type=F32,
+    )
+    aligned = aligned + (maps[0] + maps[1] + maps[2])[:, EMB : EMB + 1]
+    _, masked = gather_end(2)
+    outer = chain_of(masked)
+    out_ref[...] = small_times_wide(outer[:, :EMB], aligned) + outer[:, EMB : EMB + 1]
     for copy in point_copies + block_copies + level_copies + [next_copy]:
         copy.wait_send()
 
@@ -416,8 +437,8 @@
             pltpu.VMEM((EMB, PATCH), F32),
             pltpu.VMEM((EMB, PATCH), F32),
             pltpu.VMEM((9 * EMB, BLOCK), BF16),
-            pltpu.VMEM((EMB, 128), F32),
-            pltpu.VMEM((2, EMB, 128), F32),
+            pltpu.VMEM((EMB // 2, 2 * MAP), F32),
+            pltpu.VMEM((2, EMB // 2, 2 * MAP), F32),
             pltpu.VMEM((3, EMB, BLOCK), F32),
             pltpu.VMEM((3, EMB, BLOCK), F32),
             pltpu.VMEM((narrow_count, EMB // 2, 2 * MAP), F32),

time: 81.5 us -> 80.5 us (0.988)
  Pallas kernels: 79.8 us -> 78.8 us
    pallas_call x1, Pallas kernels: 79.8 us -> 78.8 us  [shards(): pl.pallas_call(functools.partial(kernel, wide_count, narrow_count), out_s...]
where the time goes in v3:
time: 80.5 us; the launch traced here: 80.4 us
  Pallas kernels  78.8 us (98%)
  local copies, waits for them, and re-layouts  1.57 us (2%)
    pallas_call x1, Pallas kernels, shards(): pl.pallas_call(functools.partial(kernel, wide_count, narrow_count), out_s...  78.8 us

profile of v3, /device:TPU:1, one launch (start us, length us, event | category | flops | bytes accessed | tf_op | source)
XLA Modules:
  0.0 80.4 jit_solution(13195268840415866236)
XLA Ops:
  0.0 78.8 %shard_map.28 = f32[32,1024]{1,0:T(8,128)} custom-call(f32[1024,128]{1,0:T(8,128)} %points_ref.1, f32[32,3072]{1,0:T(8,128)} %start_ref.1), custom_call_target="tpu_custom_call" | custom-call | tf_op jit(solution)/shard_map/pallas_call | solution.py:425
  78.8 1.6 %copy.4 = f32[32,1024]{1,0:T(8,128)} copy(f32[32,1024]{1,0:T(8,128)} %shard_map.28) | data formatting | bytes 262144

commit v4 on v3

--- a/solution.py
+++ b/solution.py
@@ -14,13 +14,15 @@
 PATCH = 3 * BLOCK
 ITERS = 4
 NS_STEPS = 16
-CHUNKS = 4
-CHUNK = BLOCK // CHUNKS
+CHUNKS = (256, 256, 256, 128, 128)
 MAP = 64
 LOW = 8
 
 F32 = jnp.float32
 BF16 = jnp.bfloat16
+F8 = jnp.float8_e4m3fn
+LOW_SCALE = 65536.0
+F8_MAX = 448.0
 NT = (((1,), (1,)), ((), ()))
 HIGHEST = lax.Precision.HIGHEST
 MESH = pl.DeviceIdType.MESH
@@ -39,7 +41,7 @@
     return high, middle, (rest - middle.astype(F32)).astype(BF16)
 
 
-def prepare(rows, left_ref, right_ref, at):
+def prepare(rows, left_ref, right_ref, weight_ref, weights_ref, at):
     count = rows.shape[0]
     scaled = rows * SCALE
     high, low = halves(scaled)
@@ -56,6 +58,7 @@
     left_ref[here, DIM : 2 * DIM] = low
     left_ref[here, 2 * DIM : 3 * DIM] = high
     left_ref[here, 3 * DIM : 4 * DIM] = tail.astype(BF16)
+    weight_ref[here, :] = jnp.broadcast_to(jnp.exp2(norms), (count, 128))
     turned = scaled.T
     high, low = halves(turned)
     norms = -0.5 * jnp.sum(turned * turned, axis=0, keepdims=True)
@@ -70,13 +73,17 @@
     right_ref[DIM : 2 * DIM, here] = high
     right_ref[2 * DIM : 3 * DIM, here] = low
     right_ref[3 * DIM : 4 * DIM, here] = tail.astype(BF16)
-
-
-def kernel_tile(left_ref, right_ref, high_ref, low_ref, rows, cols):
+    weights_ref[:, here] = jnp.exp2(norms)
+
+
+def kernel_tile(left_ref, right_ref, weight_ref, weights_ref, high_ref, low_ref, rows, cols):
     power = jnp.dot(left_ref[rows, :], right_ref[:, cols], preferred_element_type=F32)
-    high, low = halves(jnp.exp2(power))
+    repeats = (cols.stop - cols.start) // 128
+    value = jnp.exp2(power) - jnp.tile(weight_ref[rows, :], (1, repeats)) * weights_ref[:, cols]
+    high = value.astype(BF16)
+    rest = (value - high.astype(F32)) * LOW_SCALE
     high_ref[rows, cols] = high
-    low_ref[rows, cols] = low
+    low_ref[rows, cols] = jnp.minimum(jnp.maximum(rest, -F8_MAX), F8_MAX).astype(F8)
 
 
 def product_nt(a, b):
@@ -146,8 +153,11 @@
     out_ref,
     own_ref,
     near_ref,
+    points,
     left_ref,
     right_ref,
+    weight_ref,
+    weights_ref,
     high_ref,
     low_ref,
     basis_ref,
@@ -161,6 +171,7 @@
     low_maps_ref,
     high_maps_ref,
     next_map_ref,
+    load_sem,
     x_send,
     x_recv,
     e_send,
@@ -198,6 +209,12 @@
         (along_lower, LOW, lower, low_maps_ref),
         (along_upper, uppers, upper, high_maps_ref),
     )
+    loads = (
+        pltpu.make_async_copy(points_ref, points, load_sem.at[0]),
+        pltpu.make_async_copy(start_ref, basis_ref, load_sem.at[1]),
+    )
+    for copy in loads:
+        copy.start()
     barrier = pltpu.get_barrier_semaphore()
     greeted = 0
     for peer in (after_id, before_id):
@@ -220,43 +237,62 @@
         )
 
     point_copies = []
-    for c in range(CHUNKS):
+    done = 0
+    for c, size in enumerate(CHUNKS):
         for side, peer in ((0, after_id), (1, before_id)):
-            at = BLOCK - (c + 1) * CHUNK if side == 0 else c * CHUNK
-            rows = points_ref.at[pl.ds(at, CHUNK), :]
+            rows = pl.ds(BLOCK - done - size if side == 0 else done, size)
             copy = remote(
-                rows, near_ref.at[c, side], x_send.at[c, side], x_recv.at[c, side], peer
+                points_ref.at[rows, :],
+                near_ref.at[side, rows, :],
+                x_send.at[c, side],
+                x_recv.at[c, side],
+                peer,
             )
             copy.start()
             point_copies.append(copy)
-
-    basis_ref[...] = start_ref[...]
-    for c in range(CHUNKS):
-        at = BLOCK + c * CHUNK
-        prepare(points_ref[c * CHUNK : (c + 1) * CHUNK, :], left_ref, right_ref, at)
-    tile = functools.partial(kernel_tile, left_ref, right_ref, high_ref, low_ref)
+        done += size
+
+    for copy in loads:
+        copy.wait()
+    origin = jnp.mean(points[...], axis=0, keepdims=True)
+    operands = (left_ref, right_ref, weight_ref, weights_ref)
+    tile = functools.partial(kernel_tile, *operands, high_ref, low_ref)
+    for at in range(0, BLOCK, 256):
+        prepare(points[at : at + 256, :] - origin, *operands, BLOCK + at)
     tile(slice(BLOCK, 2 * BLOCK), slice(BLOCK, 2 * BLOCK))
-    for c in range(CHUNKS):
-        first, last = BLOCK - c * CHUNK, 2 * BLOCK + c * CHUNK
-        known, grown = slice(first, last), slice(first - CHUNK, last + CHUNK)
-        sides = (slice(first - CHUNK, first), slice(last, last + CHUNK))
+    first, last = BLOCK, 2 * BLOCK
+    for c, size in enumerate(CHUNKS):
+        known, grown = slice(first, last), slice(first - size, last + size)
+        sides = (slice(first - size, first), slice(last, last + size))
         for side in (0, 1):
             point_copies[2 * c + side].wait_recv()
-            prepare(near_ref[c, side], left_ref, right_ref, sides[side].start)
+            at = sides[side].start
+            here = pl.ds(at - 2 * BLOCK * side, size)
+            prepare(near_ref[side, here, :] - origin, *operands, at)
         for side in (0, 1):
             tile(grown, sides[side])
             tile(sides[side], known)
+        first, last = grown.start, grown.stop
 
     def factor_and_pair():
         basis = basis_ref[...]
         factor = 0.5 * inverse_factor(product_nt(basis, basis))
-        high, low = halves(basis - jnp.mean(basis, axis=1, keepdims=True))
-        return factor, jnp.concatenate([high, low], axis=0)
-
-    def product(pair, part):
+        basis = basis - jnp.mean(basis, axis=1, keepdims=True)
+        pair = jnp.concatenate(halves(basis), axis=0)
+        weighted = jnp.sum(basis * weights_ref[...], axis=1, keepdims=True)
+        top = jnp.maximum(jnp.max(jnp.abs(basis), axis=1, keepdims=True), 1e-30)
+        small = basis * (256.0 / top)
+        small_high = small.astype(F8)
+        small_low = (small - small_high.astype(F32)).astype(F8)
+        small_pair = jnp.concatenate([small_high, small_low], axis=0)
+        return factor, (pair, small_pair, top / (256.0 * LOW_SCALE), weighted)
+
+    def product(basis, part):
+        pair, small_pair, unit, weighted = basis
         cols = slice(part * BLOCK, (part + 1) * BLOCK)
         by_high = jnp.dot(pair, high_ref[:, cols], preferred_element_type=F32)
-        by_low = jnp.dot(pair[:EMB], low_ref[:, cols], preferred_element_type=F32)
+        by_low = jnp.dot(small_pair, low_ref[:, cols], preferred_element_type=F32)
+        by_low = (by_low[:EMB] + by_low[EMB:]) * unit + weighted * weights_ref[:, cols]
         return by_high[:EMB] + (by_high[EMB:] + by_low)
 
     @pl.loop(0, ITERS - 1)
@@ -425,15 +461,18 @@
     return pl.pallas_call(
         functools.partial(kernel, wide_count, narrow_count),
         out_shape=jax.ShapeDtypeStruct((EMB, BLOCK), F32),
-        in_specs=[in_vmem, in_vmem],
+        in_specs=[pl.BlockSpec(memory_space=pl.ANY)] * 2,
         out_specs=in_vmem,
         scratch_shapes=[
             pltpu.VMEM((EMB // 2, 2 * MAP), F32),
-            pltpu.VMEM((CHUNKS, 2, CHUNK, DIM), F32),
+            pltpu.VMEM((2, BLOCK, DIM), F32),
+            pltpu.VMEM((BLOCK, DIM), F32),
             pltpu.VMEM((PATCH, 4 * DIM), BF16),
             pltpu.VMEM((4 * DIM, PATCH), BF16),
+            pltpu.VMEM((PATCH, 128), F32),
+            pltpu.VMEM((1, PATCH), F32),
             pltpu.VMEM((PATCH, PATCH), BF16),
-            pltpu.VMEM((PATCH, PATCH), BF16),
+            pltpu.VMEM((PATCH, PATCH), F8),
             pltpu.VMEM((EMB, PATCH), F32),
             pltpu.VMEM((EMB, PATCH), F32),
             pltpu.VMEM((9 * EMB, BLOCK), BF16),
@@ -445,8 +484,9 @@
             pltpu.VMEM((LOW, EMB // 2, 2 * MAP), F32),
             pltpu.VMEM((wide_count // LOW, EMB // 2, 2 * MAP), F32),
             pltpu.VMEM((EMB // 2, 2 * MAP), F32),
-            pltpu.SemaphoreType.DMA((CHUNKS, 2)),
-            pltpu.SemaphoreType.DMA((CHUNKS, 2)),
+            pltpu.SemaphoreType.DMA((2,)),
+            pltpu.SemaphoreType.DMA((len(CHUNKS), 2)),
+            pltpu.SemaphoreType.DMA((len(CHUNKS), 2)),
             pltpu.SemaphoreType.DMA((3,)),
             pltpu.SemaphoreType.DMA((3,)),
             pltpu.SemaphoreType.DMA((2,)),

time: 80.5 us -> 77 us (0.957)
  Pallas kernels: 78.8 us -> 75.4 us
    pallas_call x1, Pallas kernels: 78.8 us -> 75.4 us  [shards(): pl.pallas_call(functools.partial(kernel, wide_count, narrow_count), out_s...]
where the time goes in v4:
time: 77 us
  Pallas kernels  75.4 us (98%)
  local copies, waits for them, and re-layouts  1.57 us (2%)
    pallas_call x1, Pallas kernels, shards(): pl.pallas_call(functools.partial(kernel, wide_count, narrow_count), out_s...  75.4 us
    unnamed x1, local copies, waits for them, and re-layouts  1.57 us

profile of v4, /device:TPU:1, one launch (start us, length us, event | category | flops | bytes accessed | tf_op | source)
XLA Modules:
  0.0 77.0 jit_solution(2755051008424045732)
XLA Ops:
  0.0 75.4 %shard_map.28 = f32[32,1024]{1,0:T(8,128)} custom-call(f32[1024,128]{1,0:T(8,128)} %points_ref.1, f32[32,3072]{1,0:T(8,128)} %start_ref.1), custom_call_target="tpu_custom_call" | custom-call | tf_op jit(solution)/shard_map/pallas_call | solution.py:461
  75.4 1.6 %copy.4 = f32[32,1024]{1,0:T(8,128)} copy(f32[32,1024]{1,0:T(8,128)} %shard_map.28) | data formatting | bytes 262144

commit v5 on v4

--- a/solution.py
+++ b/solution.py
@@ -14,7 +14,7 @@
 PATCH = 3 * BLOCK
 ITERS = 4
 NS_STEPS = 16
-CHUNKS = (256, 256, 256, 128, 128)
+CHUNKS = (256, 256, 256, 256)
 MAP = 64
 LOW = 8
 
@@ -94,15 +94,26 @@
     return full[:rows, :rows] + (full[:rows, rows:] + full[rows:, :rows]) + full[rows:, rows:]
 
 
-def inverse_factor(gram):
+def elimination(gram):
     n = gram.shape[0]
     lane = lax.broadcasted_iota(jnp.int32, (n, 128), 1)
     row = lax.broadcasted_iota(jnp.int32, (n, 128), 0)
     both = jnp.concatenate([gram, jnp.zeros((n, 128 - n), F32)], axis=1)
-    both = jnp.where(lane == row + n, 1.0, both)
-    for k in range(n - 1):
+    return jnp.where(lane == row + n, 1.0, both)
+
+
+def eliminated(both, columns):
+    row = lax.broadcasted_iota(jnp.int32, both.shape, 0)
+    for k in columns:
         pivot = both[k : k + 1, :] / both[k : k + 1, k : k + 1]
         both = jnp.where(row > k, both - both[:, k : k + 1] * pivot, both)
+    return both
+
+
+def inverse_factor(both):
+    n = both.shape[0]
+    lane = lax.broadcasted_iota(jnp.int32, both.shape, 1)
+    row = lax.broadcasted_iota(jnp.int32, both.shape, 0)
     diagonal = jnp.sum(jnp.where(lane == row, both, 0.0), axis=1, keepdims=True)
     return both[:, n : 2 * n] / jnp.sqrt(diagonal)
 
@@ -236,6 +247,12 @@
             device_id_type=MESH,
         )
 
+    def start_now(copies):
+        @pl.when(me >= 0)
+        def _():
+            for copy in copies:
+                copy.start()
+
     point_copies = []
     done = 0
     for c, size in enumerate(CHUNKS):
@@ -274,9 +291,9 @@
             tile(sides[side], known)
         first, last = grown.start, grown.stop
 
-    def factor_and_pair():
+    def elimination_and_basis():
         basis = basis_ref[...]
-        factor = 0.5 * inverse_factor(product_nt(basis, basis))
+        both = elimination(product_nt(basis, basis))
         basis = basis - jnp.mean(basis, axis=1, keepdims=True)
         pair = jnp.concatenate(halves(basis), axis=0)
         weighted = jnp.sum(basis * weights_ref[...], axis=1, keepdims=True)
@@ -285,7 +302,7 @@
         small_high = small.astype(F8)
         small_low = (small - small_high.astype(F32)).astype(F8)
         small_pair = jnp.concatenate([small_high, small_low], axis=0)
-        return factor, (pair, small_pair, top / (256.0 * LOW_SCALE), weighted)
+        return both, (pair, small_pair, top / (256.0 * LOW_SCALE), weighted)
 
     def product(basis, part):
         pair, small_pair, unit, weighted = basis
@@ -297,20 +314,24 @@
 
     @pl.loop(0, ITERS - 1)
     def _(_):
-        factor, pair = factor_and_pair()
+        both, basis = elimination_and_basis()
+        factor = 0.5 * inverse_factor(eliminated(both, range(EMB - 1)))
         for part in range(3):
-            image_ref[:, part * BLOCK : (part + 1) * BLOCK] = product(pair, part)
+            image_ref[:, part * BLOCK : (part + 1) * BLOCK] = product(basis, part)
         image = image_ref[...]
         image = image - jnp.mean(image, axis=1, keepdims=True)
         basis_ref[...] = small_times_wide(factor, image)
 
-    factor, pair = factor_and_pair()
+    both, basis = elimination_and_basis()
     block_copies = []
-    for part, peer in ((1, after_id), (2, after_id), (0, before_id)):
-        send_ref[part] = product(pair, part)
+    thirds_of_steps = (range(0, 11), range(11, 21), range(21, EMB - 1))
+    for steps, part, peer in zip(thirds_of_steps, (1, 2, 0), (after_id, after_id, before_id)):
+        both = eliminated(both, steps)
+        send_ref[part] = product(basis, part)
         copy = remote(send_ref.at[part], got_ref.at[part], e_send.at[part], e_recv.at[part], peer)
-        copy.start()
+        start_now([copy])
         block_copies.append(copy)
+    factor = 0.5 * inverse_factor(both)
     raw = jnp.concatenate([send_ref[0], send_ref[1], send_ref[2]], axis=1)
     raw_mean = jnp.mean(raw, axis=1, keepdims=True)
     image = small_times_wide(factor, raw - raw_mean)
@@ -325,8 +346,8 @@
         copy = remote(
             stats_ref, near_stats_ref.at[side], s_send.at[side], s_recv.at[side], peer
         )
-        copy.start()
         block_copies.append(copy)
+    start_now(block_copies[3:])
     image_ref[:, : 2 * BLOCK] = image[:, : 2 * BLOCK] * scale
 
     source = image_ref[:, : 2 * BLOCK]
@@ -388,8 +409,8 @@
                 m_recv.at[slots[level] + step - 1],
                 peer_at(step),
             )
-            copy.start()
             copies.append(copy)
+        start_now(copies)
         return copies
 
     def gather_end(level):
@@ -414,7 +435,7 @@
     own_ref[...] = packed(own_map)
     level_copies = gather_start(0, own_map)
     next_copy = remote(own_ref, next_map_ref, n_send, n_recv, before_id)
-    next_copy.start()
+    start_now([next_copy])
     block_copies[2].wait_recv()
     block_copies[4].wait_recv()
     next_stats = unpacked(near_stats_ref[1])

time: 77 us -> 75 us (0.974)
  Pallas kernels: 75.4 us -> 73.4 us
    pallas_call x1, Pallas kernels: 75.4 us -> 73.4 us  [shards(): pl.pallas_call(functools.partial(kernel, wide_count, narrow_count), out_s...]
where the time goes in v5:
time: 75 us; the launch traced here: 74.9 us
  Pallas kernels  73.4 us (98%)
  local copies, waits for them, and re-layouts  1.57 us (2%)
    pallas_call x1, Pallas kernels, shards(): pl.pallas_call(functools.partial(kernel, wide_count, narrow_count), out_s...  73.4 us
    unnamed x1, local copies, waits for them, and re-layouts  1.57 us

profile of v5, /device:TPU:1, one launch (start us, length us, event | category | flops | bytes accessed | tf_op | source)
XLA Modules:
  0.0 74.9 jit_solution(15808370128976888912)
XLA Ops:
  0.0 73.4 %shard_map.28 = f32[32,1024]{1,0:T(8,128)} custom-call(f32[1024,128]{1,0:T(8,128)} %points_ref.1, f32[32,3072]{1,0:T(8,128)} %start_ref.1), custom_call_target="tpu_custom_call" | custom-call | tf_op jit(solution)/shard_map/pallas_call | solution.py:482
  73.4 1.6 %copy.4 = f32[32,1024]{1,0:T(8,128)} copy(f32[32,1024]{1,0:T(8,128)} %shard_map.28) | data formatting | bytes 262144

commit v6 on v5

--- a/solution.py
+++ b/solution.py
@@ -80,6 +80,11 @@
     power = jnp.dot(left_ref[rows, :], right_ref[:, cols], preferred_element_type=F32)
     repeats = (cols.stop - cols.start) // 128
     value = jnp.exp2(power) - jnp.tile(weight_ref[rows, :], (1, repeats)) * weights_ref[:, cols]
+    keep(value, high_ref, low_ref, rows, cols)
+    return value
+
+
+def keep(value, high_ref, low_ref, rows, cols):
     high = value.astype(BF16)
     rest = (value - high.astype(F32)) * LOW_SCALE
     high_ref[rows, cols] = high
@@ -279,17 +284,17 @@
     tile(slice(BLOCK, 2 * BLOCK), slice(BLOCK, 2 * BLOCK))
     first, last = BLOCK, 2 * BLOCK
     for c, size in enumerate(CHUNKS):
-        known, grown = slice(first, last), slice(first - size, last + size)
-        sides = (slice(first - size, first), slice(last, last + size))
         for side in (0, 1):
             point_copies[2 * c + side].wait_recv()
-            at = sides[side].start
+            known = slice(first, last)
+            added = slice(first - size, first) if side == 0 else slice(last, last + size)
+            at = added.start
             here = pl.ds(at - 2 * BLOCK * side, size)
             prepare(near_ref[side, here, :] - origin, *operands, at)
-        for side in (0, 1):
-            tile(grown, sides[side])
-            tile(sides[side], known)
-        first, last = grown.start, grown.stop
+            first, last = min(first, added.start), max(last, added.stop)
+            value = tile(slice(first, last), added)
+            value = value[known.start - first : known.stop - first].T
+            keep(value, high_ref, low_ref, added, known)
 
     def elimination_and_basis():
         basis = basis_ref[...]

time: 75 us -> 75.7 us (level)
  no operation moved by 1% of the time
where the time goes in v6:
time: 75.7 us; the launch traced here: 75.6 us
  Pallas kernels  74 us (98%)
  local copies, waits for them, and re-layouts  1.57 us (2%)
    pallas_call x1, Pallas kernels, shards(): pl.pallas_call(functools.partial(kernel, wide_count, narrow_count), out_s...  74 us
    unnamed x1, local copies, waits for them, and re-layouts  1.57 us

profile of v6, /device:TPU:1, one launch (start us, length us, event | category | flops | bytes accessed | tf_op | source)
XLA Modules:
  0.0 75.6 jit_solution(16576904532043923072)
XLA Ops:
  0.0 74.0 %shard_map.28 = f32[32,1024]{1,0:T(8,128)} custom-call(f32[1024,128]{1,0:T(8,128)} %points_ref.1, f32[32,3072]{1,0:T(8,128)} %start_ref.1), custom_call_target="tpu_custom_call" | custom-call | tf_op jit(solution)/shard_map/pallas_call | solution.py:487
  74.0 1.6 %copy.4 = f32[32,1024]{1,0:T(8,128)} copy(f32[32,1024]{1,0:T(8,128)} %shard_map.28) | data formatting | bytes 262144

commit v7 on v5

--- a/solution.py
+++ b/solution.py
@@ -80,6 +80,11 @@
     power = jnp.dot(left_ref[rows, :], right_ref[:, cols], preferred_element_type=F32)
     repeats = (cols.stop - cols.start) // 128
     value = jnp.exp2(power) - jnp.tile(weight_ref[rows, :], (1, repeats)) * weights_ref[:, cols]
+    keep(value, high_ref, low_ref, rows, cols)
+    return value
+
+
+def keep(value, high_ref, low_ref, rows, cols):
     high = value.astype(BF16)
     rest = (value - high.astype(F32)) * LOW_SCALE
     high_ref[rows, cols] = high
@@ -287,8 +292,8 @@
             here = pl.ds(at - 2 * BLOCK * side, size)
             prepare(near_ref[side, here, :] - origin, *operands, at)
         for side in (0, 1):
-            tile(grown, sides[side])
-            tile(sides[side], known)
+            value = tile(grown, sides[side])[size : size + last - first].T
+            keep(value, high_ref, low_ref, sides[side], known)
         first, last = grown.start, grown.stop
 
     def elimination_and_basis():

time: 75 us -> 74.1 us (0.988)
  Pallas kernels: 73.4 us -> 72.4 us
    pallas_call x1, Pallas kernels: 73.4 us -> 72.4 us  [shards(): pl.pallas_call(functools.partial(kernel, wide_count, narrow_count), out_s...]
where the time goes in v7:
time: 74.1 us; the launch traced here: 74 us
  Pallas kernels  72.4 us (98%)
  local copies, waits for them, and re-layouts  1.57 us (2%)
    pallas_call x1, Pallas kernels, shards(): pl.pallas_call(functools.partial(kernel, wide_count, narrow_count), out_s...  72.4 us
    unnamed x1, local copies, waits for them, and re-layouts  1.57 us

profile of v7, /device:TPU:1, one launch (start us, length us, event | category | flops | bytes accessed | tf_op | source)
XLA Modules:
  0.0 74.0 jit_solution(11715201986060836130)
XLA Ops:
  0.0 72.4 %shard_map.28 = f32[32,1024]{1,0:T(8,128)} custom-call(f32[1024,128]{1,0:T(8,128)} %points_ref.1, f32[32,3072]{1,0:T(8,128)} %start_ref.1), custom_call_target="tpu_custom_call" | custom-call | tf_op jit(solution)/shard_map/pallas_call | solution.py:487
  72.4 1.6 %copy.4 = f32[32,1024]{1,0:T(8,128)} copy(f32[32,1024]{1,0:T(8,128)} %shard_map.28) | data formatting | bytes 262144
